TPU v7x, 128 devices: a whole 4x4x4 slice. The times are simulated.
128 devices in a mesh: layer: 2 (over core), prow: 4 (over x), pcol: 16 (over z, y).
Axes of the slice: x: 4, y: 4, z: 4, core: 2. Of those that a mesh axis runs over, the one named last changes fastest.
Arguments:
- stored_inverse: bfloat16 [8192, 8192], P('prow', 'pcol'), may hold values from -4 to 64, as said below
- lhat: bfloat16 [2, 4096, 256], P('layer', ('prow', 'pcol')), may hold values from -0.25 to 0.25
- diag_inverse: bfloat16 [2, 2, 256, 256], P('layer'), may hold values from -6 to 6
- ancestors: int32 [2, 2, 8], P('layer'), may hold values from 0 to 29, as said below
Outputs:
- column_blocks: bfloat16 [2, 8192, 512], P('layer', 'prow')
- row_blocks: bfloat16 [2, 8192, 512], P('layer', 'pcol')
- diag_blocks: bfloat16 [2, 2, 256, 256], P('layer')
Inputs may be any that keep to these rules, and one draw needn't show every extreme that they name: `stored_inverse`: Symmetric; every tile whose row or column block index is 28 or more is zero. `ancestors`: each list holds 8 distinct block indices in increasing order. At level 0 they are below 28. At level l >= 1 the list of a supernode is its parent's list (the parent is a supernode of level l - 1) with one entry removed, followed by the parent's own block; every supernode of level l - 1 is the parent of exactly one supernode of level l.
All inputs are finite; a program needn't handle non-finite values.
Results may differ from a plain program's by a relative error of at most 0.018.
Values may be sent and summed in bfloat16 or wider, within the bound.
A program may use at most 128 MiB of HBM per device.

v0:
```python
import jax
import jax.numpy as jnp
from jax import lax
from jax.sharding import PartitionSpec as P

BLOCK = 256
ANCESTORS = 8
SUPERS = 2


def passed_along(block, axis, distance):
    devices = range(lax.axis_size(axis))
    route = [(i - distance, i) for i in devices if i - distance in devices]
    return lax.ppermute(block, axis, route)


def place_panels(panel_tiles, anc_level, block_ids):
    onehot = (anc_level[:, :, None] == block_ids[None, None, :]).astype(jnp.bfloat16)
    placed = jnp.einsum("kpm,kpxy->mxky", onehot, panel_tiles, preferred_element_type=jnp.float32)
    block_total = block_ids.shape[0]
    return placed.astype(jnp.bfloat16).reshape(block_total * BLOCK, panel_tiles.shape[0] * BLOCK)


def masked_share(share_sum, anc_level, first_row, block_ids):
    share_rows = share_sum.shape[0]
    supers = anc_level.shape[0]
    positions = (first_row + jnp.arange(share_rows, dtype=jnp.int32)) // BLOCK
    member = jnp.any(anc_level[:, :, None] == block_ids[None, None, :], axis=1)
    picked = jnp.take(member, positions, axis=1)
    keep_rows = picked.T[:, :, None]
    shaped = share_sum.reshape(share_rows, supers, BLOCK)
    return (
        jnp.where(keep_rows, -shaped, 0.0).astype(jnp.bfloat16).reshape(share_rows, supers * BLOCK)
    )


def diag_part(panel_share, x_share, supers):
    share_rows = x_share.shape[0]
    return jnp.einsum(
        "xky,xkz->kyz",
        panel_share.reshape(share_rows, supers, BLOCK),
        x_share.reshape(share_rows, supers, BLOCK),
        preferred_element_type=jnp.float32,
    )


def insert_level(stored, x_rows, y_cols, diag_new, level_blocks, row_ids, col_ids):
    row_total = row_ids.shape[0]
    col_total = col_ids.shape[0]
    supers = diag_new.shape[0]
    tile_grid = stored.reshape(row_total, BLOCK, col_total, BLOCK)
    x_tiles = x_rows.reshape(row_total, BLOCK, supers, BLOCK)
    y_tiles = y_cols.reshape(col_total, BLOCK, supers, BLOCK)
    for super_id in range(supers):
        target = level_blocks[super_id]
        col_hit = (col_ids == target)[None, None, :, None]
        row_hit = (row_ids == target)[:, None, None, None]
        tile_grid = jnp.where(col_hit, x_tiles[:, :, super_id, :][:, :, None, :], tile_grid)
        across = jnp.transpose(y_tiles[:, :, super_id, :], (2, 0, 1))[None]
        tile_grid = jnp.where(row_hit, across, tile_grid)
        tile_grid = jnp.where(row_hit & col_hit, diag_new[super_id][None, :, None, :], tile_grid)
    return tile_grid.reshape(stored.shape)


def body(stored_inverse, lhat, diag_inverse, ancestors):
    layer_procs = lax.axis_size("layer")
    row_procs = lax.axis_size("prow")
    col_procs = lax.axis_size("pcol")
    layer_id = lax.axis_index("layer")
    row_id = lax.axis_index("prow")
    col_id = lax.axis_index("pcol")
    row_total = stored_inverse.shape[0] // BLOCK
    col_total = stored_inverse.shape[1] // BLOCK
    row_ids = row_id * row_total + jnp.arange(row_total, dtype=jnp.int32)
    col_ids = col_id * col_total + jnp.arange(col_total, dtype=jnp.int32)
    top_blocks = row_procs * row_total - layer_procs * SUPERS
    panel_width = SUPERS * BLOCK
    super_range = jnp.arange(SUPERS, dtype=jnp.int32)
    panels = lax.all_gather(lhat, ("prow", "pcol"), axis=1, tiled=True)
    rows_out = jnp.zeros((1, row_total * BLOCK, panel_width), jnp.bfloat16)
    cols_out = jnp.zeros((1, col_total * BLOCK, panel_width), jnp.bfloat16)
    diag_out = jnp.zeros_like(diag_inverse)
    stored = stored_inverse
    panel_flat = panels[0]
    panel_tiles = panel_flat.reshape(SUPERS, ANCESTORS, BLOCK, BLOCK)
    anc_level = ancestors[0]
    level_diag = diag_inverse[0].astype(jnp.float32)
    level_blocks = top_blocks + layer_id * SUPERS + super_range
    panel_cols = place_panels(panel_tiles, anc_level, col_ids)
    panel_rows = place_panels(panel_tiles, anc_level, row_ids)
    x_share = row_total * BLOCK // col_procs
    y_share = col_total * BLOCK // row_procs
    x_first = col_id * x_share
    panel_share = lax.dynamic_slice_in_dim(panel_rows, x_first, x_share, 0)
    for level in range(layer_procs):
        row_slice = stored
        column_sum = lax.psum_scatter(
            jnp.dot(row_slice, panel_cols, preferred_element_type=jnp.float32).astype(jnp.bfloat16),
            "pcol",
            scatter_dimension=0,
            tiled=True,
        ).astype(jnp.float32)
        x_part = masked_share(column_sum, anc_level, x_first, row_ids)
        col_slice = stored
        row_sum = lax.psum_scatter(
            lax.dot_general(
                col_slice, panel_rows, (((0,), (0,)), ((), ())), preferred_element_type=jnp.float32
            ).astype(jnp.bfloat16),
            "prow",
            scatter_dimension=0,
            tiled=True,
        ).astype(jnp.float32)
        y_part = masked_share(row_sum, anc_level, row_id * y_share, col_ids)
        diag_sum = lax.psum(diag_part(panel_share, x_part, SUPERS), ("prow", "pcol"))
        diag_new = (level_diag - diag_sum).astype(jnp.bfloat16)
        x_rows = lax.all_gather(x_part, "pcol", axis=0, tiled=True)
        y_cols = lax.all_gather(y_part, "prow", axis=0, tiled=True)
        own_level = level == layer_id
        rows_out = jnp.where(own_level, x_rows[None], rows_out)
        cols_out = jnp.where(own_level, y_cols[None], cols_out)
        diag_out = jnp.where(own_level, diag_new[None], diag_out)
        stored = insert_level(stored, x_rows, y_cols, diag_new, level_blocks, row_ids, col_ids)
        if level + 1 < layer_procs:
            stored = passed_along(stored, "layer", 1)
    return (rows_out, cols_out, diag_out)


def solution(mesh):
    return jax.shard_map(
        body,
        mesh=mesh,
        in_specs=(
            P("prow", "pcol"),
            P("layer", ("prow", "pcol"), None),
            P("layer", None, None, None),
            P("layer", None, None),
        ),
        out_specs=(
            P("layer", "prow", None),
            P("layer", "pcol", None),
            P("layer", None, None, None),
        ),
        check_vma=False,
    )
```

profile of v0, /device:TPU:1, one launch (start us, length us, event | category | flops | bytes accessed | tf_op | source)
XLA Modules:
  0.0 671.6 jit_solution(3385333941184695344)
XLA Ops:
  8.0 70.9 %all-gather.4.cloned.1.call-done = bf16[1,4096,256]{2,1,0:T(8,128)(2,1)} async-done(((bf16[1,64,256]{2,1,0:T(8,128)(2,1)}), bf16[1,4096,256]{2,1,0:T(8,128)(2,1)}) %all-gather.4.cloned.1.call-update) | async-done | bytes 2097168 | tf_op jit(solution)/shard_map/all_gather | solution.py:79
  78.9 3.2 fusion.7
  84.9 2.5 copy.58
  89.1 2.7 convert_bitcast_fusion
  91.7 3.8 copy.40
  101.9 57.1 %reduce-scatter.13.cloned.1.call-done = bf16[128,512]{1,0:T(8,128)(2,1)} async-done(((bf16[2048,512]{1,0:T(8,128)(2,1)}), bf16[128,512]{1,0:T(8,128)(2,1)}) %reduce-scatter.13.cloned.1.call-update) | async-done | bytes 131088
  162.1 2.9 copy.50
  175.1 6.9 %reduce-scatter.15.cloned.1.call-done = bf16[128,512]{1,0:T(8,128)(2,1)} async-done(((bf16[512,512]{1,0:T(8,128)(2,1)}), bf16[128,512]{1,0:T(8,128)(2,1)}) %reduce-scatter.15.cloned.1.call-update) | async-done | bytes 131088
  183.0 11.8 %all_gather.16 = bf16[512,512]{0,1:T(8,128)(2,1)S(1)} all-gather(bf16[128,512]{0,1:T(8,128)(2,1)S(1)} %fusion.15), channel_id=1, replica_groups=mesh['layer'=2,'prow'=4,'pcol'=16] {'prow'}, dimensions={0}, use_global_device_ids=true | all-gather | bytes 655360 | tf_op jit(solution)/shard_map/all_gather | solution.py:117
  202.0 112.6 %all-reduce.3.cloned.1.call-done = f32[2,256,256]{2,1,0:T(8,128)} async-done(((f32[2,256,256]{2,1,0:T(8,128)}), f32[2,256,256]{2,1,0:T(8,128)}) %all-reduce.3.cloned.1.call-update) | async-done | bytes 524304 | tf_op jit(solution)/shard_map/psum | solution.py:114
  316.0 2.1 copy.71
  318.3 2.1 copy.76
  320.4 42.4 %all-gather.6.cloned.1.call-done = bf16[2048,512]{0,1:T(8,128)(2,1)} async-done(((bf16[128,512]{0,1:T(8,128)(2,1)}), bf16[2048,512]{0,1:T(8,128)(2,1)}) %all-gather.6.cloned.1.call-update) | async-done | bytes 2097168 | tf_op jit(solution)/shard_map/all_gather | solution.py:116
  362.9 2.3 copy.73
  372.4 5.2 collective-permute-done
  378.9 2.6 convolution_convert_fusion
  383.1 3.7 convolution_convert_fusion.2
  386.9 66.4 %reduce-scatter.17.cloned.1.call-done = bf16[128,512]{1,0:T(8,128)(2,1)} async-done(((bf16[2048,512]{1,0:T(8,128)(2,1)}), bf16[128,512]{1,0:T(8,128)(2,1)}) %reduce-scatter.17.cloned.1.call-update) | async-done | bytes 131088
  456.4 20.5 %reduce-scatter.19.cloned.1.call-done = bf16[128,512]{1,0:T(8,128)(2,1)} async-done(((bf16[512,512]{1,0:T(8,128)(2,1)}), bf16[128,512]{1,0:T(8,128)(2,1)}) %reduce-scatter.19.cloned.1.call-update) | async-done | bytes 131088
  478.0 11.6 %all_gather.19 = bf16[512,512]{0,1:T(8,128)(2,1)S(1)} all-gather(bf16[128,512]{0,1:T(8,128)(2,1)S(1)} %fusion.16), channel_id=1, replica_groups=mesh['layer'=2,'prow'=4,'pcol'=16] {'prow'}, dimensions={0}, use_global_device_ids=true | all-gather | bytes 655360 | tf_op jit(solution)/shard_map/all_gather | solution.py:117
  490.6 119.0 %all-reduce.5.cloned.1.call-done = f32[2,256,256]{2,1,0:T(8,128)} async-done(((f32[2,256,256]{2,1,0:T(8,128)}), f32[2,256,256]{2,1,0:T(8,128)}) %all-reduce.5.cloned.1.call-update) | async-done | bytes 524304 | tf_op jit(solution)/shard_map/psum | solution.py:114
  611.5 46.5 %all-gather.8.cloned.1.call-done = bf16[2048,512]{0,1:T(8,128)(2,1)} async-done(((bf16[128,512]{0,1:T(8,128)(2,1)}), bf16[2048,512]{0,1:T(8,128)(2,1)}) %all-gather.8.cloned.1.call-update) | async-done | bytes 2097168 | tf_op jit(solution)/shard_map/all_gather | solution.py:116
  658.0 3.2 select_bitcast_fusion
  661.2 3.9 copy.54
  (139 shorter events, 51.5 us)
Async XLA Ops:
  7.2 71.7 %all-gather.4.cloned.1.call-start = ((), (), s32[]{:S(2)}) async-start(), calls=%async_computation.4 | async-start | bytes 2129920 | tf_op jit(solution)/shard_map/all_gather | solution.py:79
  7.9 151.0 %reduce-scatter.13.cloned.1.call-start = ((), (), s32[]{:S(2)}) async-start(), calls=%async_computation.9 | async-start | bytes 2228224
  78.9 4.7 copy-start.10
  87.5 94.5 %reduce-scatter.15.cloned.1.call-start = ((), (), s32[]{:S(2)}) async-start(), calls=%async_computation.10 | async-start | bytes 655360
  95.6 2.0 copy-start.11
  99.9 214.7 %all-reduce.3.cloned.1.call-start = ((), (), s32[]{:S(2)}) async-start(), calls=%async_computation.5 | async-start | bytes 1048576 | tf_op jit(solution)/shard_map/psum | solution.py:114
  161.2 201.6 %all-gather.6.cloned.1.call-start = ((), (), s32[]{:S(2)}) async-start(), calls=%async_computation.6 | async-start | bytes 2228224 | tf_op jit(solution)/shard_map/all_gather | solution.py:116
  162.0 291.3 %reduce-scatter.17.cloned.1.call-start = ((), (), s32[]{:S(2)}) async-start(), calls=%async_computation.11 | async-start | bytes 2228224
  197.5 2.0 copy-start.12
  199.9 114.6 %copy-start.13 = (bf16[1,2,256,256]{3,2,1,0:T(8,128)(2,1)S(1)}, bf16[1,2,256,256]{3,2,1,0:T(8,128)(2,1)}, u32[]{:S(2)}) copy-start(bf16[1,2,256,256]{3,2,1,0:T(8,128)(2,1)} %param.10) | copy-start | bytes 786436
  365.4 1.6 copy-start.5
  365.4 1.8 copy-start.7
  366.1 2.0 copy-start.4
  366.1 2.3 copy-start.6
  366.3 2.8 copy-start.2
  366.3 3.4 copy-start.3
  366.3 3.4 copy-start.17
  366.3 3.4 copy-start.18
  369.7 9.2 %copy-start.15 = (bf16[64,8,2,256]{3,1,2,0:T(8,128)(2,1)S(1)}, bf16[64,8,2,256]{3,1,2,0:T(8,128)(2,1)}, u32[]{:S(2)}) copy-start(bf16[64,8,2,256]{3,1,2,0:T(8,128)(2,1)} %copy-done.14) | copy-start | bytes 1572868
  371.1 6.5 collective-permute-start
  381.6 95.3 %reduce-scatter.19.cloned.1.call-start = ((), (), s32[]{:S(2)}) async-start(), calls=%async_computation.12 | async-start | bytes 655360
  386.8 222.8 %all-reduce.5.cloned.1.call-start = ((), (), s32[]{:S(2)}) async-start(), calls=%async_computation.8 | async-start | bytes 1048576 | tf_op jit(solution)/shard_map/psum | solution.py:114
  455.6 202.4 %all-gather.8.cloned.1.call-start = ((), (), s32[]{:S(2)}) async-start(), calls=%async_computation.7 | async-start | bytes 2228224 | tf_op jit(solution)/shard_map/all_gather | solution.py:116
  489.6 168.5 %copy-start.1 = (bf16[2048,512]{0,1:T(8,128)(2,1)S(1)}, bf16[2048,512]{0,1:T(8,128)(2,1)}, u32[]{:S(2)}) copy-start(bf16[2048,512]{0,1:T(8,128)(2,1)} %all-gather.6.cloned.1.call-done) | copy-start | bytes 6291460
  (6 other events, 7.4 us)
Sparse Core Ops, SparseCore 0:
  10.9 67.9 all-gather.3
  87.6 71.2 reduce-scatter.12
  161.5 20.4 reduce-scatter.14
  187.8 126.6 all-reduce.2
  316.5 46.2 all-gather.5
  381.7 71.5 reduce-scatter.16
  456.4 20.4 reduce-scatter.18
  482.9 126.6 all-reduce.4
  611.7 46.2 all-gather.7
where the time goes:
time: 672 us
  waiting for transfers between devices  548 us (82%)
  local copies, waits for them, and re-layouts  54.5 us (8%)
  blocking collectives  23.4 us (3%)
  matrix products  16.9 us (3%)
  between operations  14.4 us (2%)
  other arithmetic  12.6 us (2%)
    psum x2, waiting for transfers between devices, body(): lax.psum(diag_part(panel_share, x_part, SUPERS), ('prow', 'pcol'))  232 us
    unnamed x13, waiting for transfers between devices  152 us
    all_gather x2, waiting for transfers between devices, body(): x_rows = lax.all_gather(x_part, 'pcol', axis=0, tiled=True)  89 us
    all_gather x1, waiting for transfers between devices, body(): panels = lax.all_gather(lhat, ('prow', 'pcol'), axis=1, tiled=True)  70.9 us
    unnamed x61, local copies, waits for them, and re-layouts  40.5 us
    all_gather x2, blocking collectives, body(): y_cols = lax.all_gather(y_part, 'prow', axis=0, tiled=True)  23.4 us
  transfers between devices with their start and end apart: 10, of which 10 were waited for; matrix products, arithmetic and copies ran while one was open for 8% of the time, Pallas kernels for 0%

commit v1 on v0

v1 whole, which is shorter than its diff:
```python
import functools

import jax
import jax.numpy as jnp
from jax import lax
from jax.experimental import pallas as pl
from jax.experimental.pallas import tpu as pltpu
from jax.sharding import PartitionSpec as P

BLOCK = 256
ANCESTORS = 8
SUPERS = 2
TOP_BLOCKS = 28
SIDE = 4
PLANE = 16
QUARTER = 64
SLOTS = SUPERS * ANCESTORS
MESH = pl.DeviceIdType.MESH
BF16 = jnp.bfloat16
F32 = jnp.float32

ROUTES = (
    (("y", "z", "x"), (0, 48), (0, 128)),
    (("x", "z", "y"), (0, 48), (128, 128)),
    (("x", "y", "z"), (48, 16), (0, 256)),
)
HOPS = (2, 1, 3)


def kernel(
    anc, anc_v, panel, g_any, dinv,
    col_out, row_out, diag_out,
    panels, g_own, g_pick, panel_t, partial, partial_in, summed, staged, moved, slots, sibling_slots,
    sibling_diag, diag_send, tiles, anc_in, anc_other,
    g_sem, anc_send, anc_recv, anc_local,
    send1, recv1, send2, recv2, x_send, x_recv, c_send, c_recv, a_send, a_recv, d_send, d_recv,
):
    layer = lax.axis_index("layer")
    x = lax.axis_index("prow")
    c = lax.axis_index("pcol")
    z = c // SIDE
    y = c % SIDE
    me = {"x": x, "y": y, "z": z}

    def device(at, on_layer=None):
        return (layer if on_layer is None else on_layer, at["x"], at["z"] * SIDE + at["y"])

    g_copy = pltpu.make_async_copy(g_any, g_own, g_sem)
    g_copy.start()

    barrier = pltpu.get_barrier_semaphore()

    def greet_plane(step, carry):
        pl.semaphore_signal(barrier, inc=1, device_id=(layer, x, (c + step) % PLANE), device_id_type=MESH)
        return carry

    def greet_line(step, carry):
        pl.semaphore_signal(barrier, inc=1, device_id=(layer, (x + step) % SIDE, c), device_id_type=MESH)
        return carry

    lax.fori_loop(1, PLANE, greet_plane, 0)
    lax.fori_loop(1, SIDE, greet_line, 0)
    pl.semaphore_signal(barrier, inc=1, device_id=(1 - layer, x, c), device_id_type=MESH)
    pl.semaphore_wait(barrier, PLANE - 1 + SIDE - 1 + 1)

    anc_copy = pltpu.make_async_remote_copy(
        src_ref=anc_v, dst_ref=anc_in, send_sem=anc_send, recv_sem=anc_recv,
        device_id=(1 - layer, x, c), device_id_type=MESH,
    )
    anc_copy.start()

    def gather_phase(buf, dims, phase, route, send, recv):
        order, rows, cols = ROUTES[route]
        index = tuple(pl.ds(0, SIDE) if d in order[:phase] else me[d] for d in dims)
        part = buf.at[index + (pl.ds(*rows), pl.ds(*cols))]
        axis = order[phase]
        copies = []
        for hop in HOPS:
            at = dict(me)
            at[axis] = (me[axis] + hop) % SIDE
            copies.append(pltpu.make_async_remote_copy(
                src_ref=part, dst_ref=part,
                send_sem=send.at[route, phase, hop - 1], recv_sem=recv.at[route, phase, hop - 1],
                device_id=device(at), device_id_type=MESH,
            ))
        return copies

    def gather(buf, dims, send, recv, beside=None):
        sent = []
        for phase in range(3):
            now = [gather_phase(buf, dims, phase, route, send, recv) for route in range(3)]
            if phase == 0:
                for copies in now:
                    for copy in copies:
                        copy.start()
            sent.append(now)
            if phase == 0 and beside is not None:
                beside()
            for route in range(3):
                for copy in sent[phase][route]:
                    copy.wait_recv()
                if phase < 2:
                    ahead = gather_phase(buf, dims, phase + 1, route, send, recv)
                    for copy in ahead:
                        copy.start()
        for now in sent:
            for copies in now:
                for copy in copies:
                    copy.wait_send()

    panels[x, z, y] = panel[0]

    def pick_blocks():
        g_copy.wait()
        for k in range(SUPERS):
            def pick(p, carry):
                at = anc[0, k, p] - x * ANCESTORS
                here = jnp.logical_and(at >= 0, at < ANCESTORS)
                block = g_own[jnp.clip(at, 0, ANCESTORS - 1)]
                block = jnp.where(here, block, jnp.zeros_like(block))
                turned = block.T
                for b in range(2):
                    for q in range(SIDE):
                        first = b * BLOCK + q * QUARTER
                        g_pick[k, p, q, b] = turned[first:first + QUARTER]
                return carry
            lax.fori_loop(0, ANCESTORS, pick, 0)

    gather(panels, ("x", "z", "y"), send1, recv1, pick_blocks)

    for k in range(SUPERS):
        total = jnp.zeros((2 * BLOCK, BLOCK), F32)
        for p in range(ANCESTORS):
            tile = panels[2 * k + p // SIDE, p % SIDE].reshape(BLOCK, BLOCK)
            total += jnp.dot(
                g_pick[k, p].reshape(2 * BLOCK, BLOCK), tile, preferred_element_type=F32
            )
        partial[:, k] = total.astype(BF16).reshape(SIDE, 2, QUARTER, BLOCK)

    x_copies = []
    for hop in HOPS:
        to = (x + hop) % SIDE
        x_copies.append(pltpu.make_async_remote_copy(
            src_ref=partial.at[to], dst_ref=partial_in.at[hop - 1],
            send_sem=x_send.at[hop - 1], recv_sem=x_recv.at[hop - 1],
            device_id=(layer, to, c), device_id_type=MESH,
        ))
    for copy in x_copies:
        copy.start()
    for k in range(SUPERS):
        def turn(p, carry):
            panel_t[k, p] = panels[2 * k + p // SIDE, p % SIDE].reshape(BLOCK, BLOCK).T
            return carry
        lax.fori_loop(0, ANCESTORS, turn, 0)
    for copy in x_copies:
        copy.wait_recv()
    total = partial[x].astype(F32)
    for hop in HOPS:
        total += partial_in[hop - 1].astype(F32)
    summed[...] = total.astype(BF16)

    for s in range(SLOTS):
        at = jnp.clip(anc[0, s // ANCESTORS, s % ANCESTORS] - 2 * c, 0, 1)
        staged[s] = summed[s // ANCESTORS, at]

    def to_slot(step):
        to = (c + step) % PLANE
        return pltpu.make_async_remote_copy(
            src_ref=staged.at[to], dst_ref=moved.at[c],
            send_sem=c_send.at[step], recv_sem=c_recv.at[step],
            device_id=(layer, x, to), device_id_type=MESH,
        )

    def start_slot(step, carry):
        to_slot(step).start()
        return carry

    def wait_slot(step, carry):
        to_slot(step).wait_recv()
        return carry

    lax.fori_loop(1, PLANE, start_slot, 0)
    moved[c] = staged[c]
    lax.fori_loop(1, PLANE, wait_slot, 0)
    holder = anc[0, c // ANCESTORS, c % ANCESTORS] // 2
    slots[z, y, x] = moved[holder]
    gather(slots, ("z", "y", "x"), send2, recv2)

    a_copy = pltpu.make_async_remote_copy(
        src_ref=slots, dst_ref=sibling_slots, send_sem=a_send, recv_sem=a_recv,
        device_id=(1 - layer, x, c), device_id_type=MESH,
    )
    d_copy = pltpu.make_async_remote_copy(
        src_ref=diag_send, dst_ref=sibling_diag, send_sem=d_send, recv_sem=d_recv,
        device_id=(1 - layer, x, c), device_id_type=MESH,
    )
    anc_copy.wait_recv()
    to_smem = pltpu.make_async_copy(anc_in, anc_other, anc_local)
    to_smem.start()
    to_smem.wait()

    def slot_tile(ref, s):
        return ref[s // SIDE, s % SIDE].reshape(BLOCK, BLOCK)

    @pl.when(layer == 0)
    def _():
        a_copy.start()
        for k in range(SUPERS):
            total = dinv[0, k].astype(F32)
            for q in range(ANCESTORS):
                total += jnp.dot(
                    panel_t[k, q], slot_tile(slots, k * ANCESTORS + q), preferred_element_type=F32
                )
            diag_send[k] = total.astype(BF16)
            diag_out[0, k] = total.astype(BF16)
        d_copy.start()
        for k in range(SUPERS):
            for q in range(ANCESTORS):
                tiles[k, q] = -slot_tile(slots, k * ANCESTORS + q)
            tiles[k, ANCESTORS] = jnp.zeros((BLOCK, BLOCK), BF16)
        a_copy.wait_send()
        d_copy.wait_send()

    @pl.when(layer == 1)
    def _():
        a_copy.wait_recv()
        last = ANCESTORS - 1
        turned_sum = []
        for k in range(SUPERS):
            parent = jnp.clip(anc[0, k, last] - TOP_BLOCKS, 0, SUPERS - 1)
            edge = panels[2 * k + 1, SIDE - 1].reshape(BLOCK, BLOCK)
            total = jnp.zeros((BLOCK, BLOCK), F32)
            for q in range(last):
                block = anc[0, k, q]
                at = jnp.int32(0)
                for j in range(ANCESTORS):
                    at = jnp.where(anc_other[0, parent, j] == block, j, at)
                s = parent * ANCESTORS + at
                tile = sibling_slots[s // SIDE, s % SIDE].reshape(BLOCK, BLOCK)
                total += jnp.dot(panel_t[k, q], tile, preferred_element_type=F32)
                new = jnp.dot(tile, edge, preferred_element_type=F32)
                tiles[k, q] = (new - slot_tile(slots, k * ANCESTORS + q).astype(F32)).astype(BF16)
            turned_sum.append(total.T)
        d_copy.wait_recv()
        for k in range(SUPERS):
            parent = jnp.clip(anc[0, k, last] - TOP_BLOCKS, 0, SUPERS - 1)
            edge = panels[2 * k + 1, SIDE - 1].reshape(BLOCK, BLOCK)
            above = sibling_diag[parent]
            tiles[k, last] = (
                turned_sum[k] - jnp.dot(above, edge, preferred_element_type=F32)
            ).astype(BF16)
            tiles[k, ANCESTORS] = (
                turned_sum[k] - jnp.dot(above.T, edge, preferred_element_type=F32)
            ).astype(BF16)
            total = dinv[0, k].astype(F32)
            for q in range(ANCESTORS):
                total -= jnp.dot(panel_t[k, q], tiles[k, q], preferred_element_type=F32)
            diag_out[0, k] = total.astype(BF16)

    def place(out, first, blocks, row_side):
        for k in range(SUPERS):
            def put(j, carry):
                at = jnp.int32(0)
                hit = jnp.int32(0)
                for q in range(ANCESTORS):
                    same = anc[0, k, q] == first + j
                    at = jnp.where(same, q, at)
                    hit = jnp.where(same, 1, hit)
                if row_side:
                    turned = jnp.logical_and(layer == 1, at == ANCESTORS - 1)
                    at = jnp.where(turned, ANCESTORS, at)
                tile = tiles[k, at]
                start = pl.multiple_of(j * BLOCK, BLOCK)
                out[0, pl.ds(start, BLOCK), k * BLOCK:(k + 1) * BLOCK] = jnp.where(
                    hit > 0, tile, jnp.zeros_like(tile)
                )
                return carry
            lax.fori_loop(0, blocks, put, 0)

    place(col_out, x * ANCESTORS, ANCESTORS, False)
    place(row_out, c * 2, 2, True)

    anc_copy.wait_send()
    for copy in x_copies:
        copy.wait_send()

    def sent_slot(step, carry):
        to_slot(step).wait_send()
        return carry

    lax.fori_loop(1, PLANE, sent_slot, 0)


def body(stored_inverse, lhat, diag_inverse, ancestors):
    rows, cols = stored_inverse.shape
    stored = stored_inverse.reshape(rows // BLOCK, BLOCK, cols)
    vmem = pl.BlockSpec(memory_space=pltpu.VMEM)
    dma = pltpu.SemaphoreType.DMA
    width = SUPERS * BLOCK
    return pl.pallas_call(
        kernel,
        out_shape=(
            jax.ShapeDtypeStruct((1, rows, width), BF16),
            jax.ShapeDtypeStruct((1, cols, width), BF16),
            jax.ShapeDtypeStruct(diag_inverse.shape, BF16),
        ),
        in_specs=[pl.BlockSpec(memory_space=pltpu.SMEM), vmem, vmem, pl.BlockSpec(memory_space=pl.ANY), vmem],
        out_specs=(vmem, vmem, vmem),
        scratch_shapes=[
            pltpu.VMEM((SIDE, SIDE, SIDE, QUARTER, BLOCK), BF16),
            pltpu.VMEM((rows // BLOCK, BLOCK, cols), BF16),
            pltpu.VMEM((SUPERS, ANCESTORS, SIDE, 2, QUARTER, BLOCK), BF16),
            pltpu.VMEM((SUPERS, ANCESTORS, BLOCK, BLOCK), BF16),
            pltpu.VMEM((SIDE, SUPERS, 2, QUARTER, BLOCK), BF16),
            pltpu.VMEM((SIDE - 1, SUPERS, 2, QUARTER, BLOCK), BF16),
            pltpu.VMEM((SUPERS, 2, QUARTER, BLOCK), BF16),
            pltpu.VMEM((SLOTS, QUARTER, BLOCK), BF16),
            pltpu.VMEM((PLANE, QUARTER, BLOCK), BF16),
            pltpu.VMEM((SIDE, SIDE, SIDE, QUARTER, BLOCK), BF16),
            pltpu.VMEM((SIDE, SIDE, SIDE, QUARTER, BLOCK), BF16),
            pltpu.VMEM((SUPERS, BLOCK, BLOCK), BF16),
            pltpu.VMEM((SUPERS, BLOCK, BLOCK), BF16),
            pltpu.VMEM((SUPERS, ANCESTORS + 1, BLOCK, BLOCK), BF16),
            pltpu.VMEM((1, SUPERS, ANCESTORS), jnp.int32),
            pltpu.SMEM((1, SUPERS, ANCESTORS), jnp.int32),
            dma, dma, dma, dma,
            dma((3, 3, 3)), dma((3, 3, 3)), dma((3, 3, 3)), dma((3, 3, 3)),
            dma((3,)), dma((3,)), dma((PLANE,)), dma((PLANE,)),
            dma, dma, dma, dma,
        ],
        compiler_params=pltpu.CompilerParams(
            collective_id=0, has_side_effects=True, vmem_limit_bytes=48 << 20
        ),
        name="selected_inverse",
    )(ancestors, ancestors, lhat, stored, diag_inverse)


def solution(mesh):
    return jax.shard_map(
        body,
        mesh=mesh,
        in_specs=(
            P("prow", "pcol"),
            P("layer", ("prow", "pcol"), None),
            P("layer", None, None, None),
            P("layer", None, None),
        ),
        out_specs=(
            P("layer", "prow", None),
            P("layer", "pcol", None),
            P("layer", None, None, None),
        ),
        check_vma=False,
    )
```

time: 672 us -> 79.1 us (0.12)
  waiting for transfers between devices: 548 us -> 0 us
  Pallas kernels: 0 us -> 71.4 us
  local copies, waits for them, and re-layouts: 54.5 us -> 6.79 us
  blocking collectives: 23.4 us -> 0 us
  matrix products: 16.9 us -> 0 us
  between operations: 14.4 us -> 0.65 us
  other arithmetic: 12.6 us -> 0 us
    psum x2 -> x0, waiting for transfers between devices: 232 us -> none  [body(): lax.psum(diag_part(panel_share, x_part, SUPERS), ('prow', 'pcol'))]
    all_gather x3 -> x0, waiting for transfers between devices: 160 us -> none  [the longest x2 89 us: body(): x_rows = lax.all_gather(x_part, 'pcol', axis=0, tiled=True)]
    unnamed x13 -> x0, waiting for transfers between devices: 152 us -> none
    pallas_call x0 -> x1, Pallas kernels: none -> 71.4 us  [body(): pl.pallas_call(kernel, out_shape=(jax.ShapeDtypeStruct((1, rows, width),...]
    unnamed x61 -> x11, local copies, waits for them, and re-layouts: 40.5 us -> 6.79 us
    all_gather x2 -> x0, blocking collectives: 23.4 us -> none  [body(): y_cols = lax.all_gather(y_part, 'prow', axis=0, tiled=True)]
    dot_general x8 -> x0, matrix products: 16.9 us -> none  [the longest x2 5.87 us: place_panels(): jnp.einsum('kpm,kpxy->mxky', onehot, panel_tiles, preferred_element_type=...]
  transfers between devices with their start and end apart: 10 -> 0, of which waited for: 10 -> 0; matrix products, arithmetic and copies ran while one was open for 8% -> 0% of each run, Pallas kernels for 0% -> 0%
where the time goes in v1:
time: 79.1 us; the launch traced here: 78.8 us
  Pallas kernels  71.4 us (90%)
  local copies, waits for them, and re-layouts  6.79 us (9%)
    pallas_call x1, Pallas kernels, body(): pl.pallas_call(kernel, out_shape=(jax.ShapeDtypeStruct((1, rows, width),...  71.4 us
    unnamed x11, local copies, waits for them, and re-layouts  6.79 us

profile of v1, /device:TPU:1, one launch (start us, length us, event | category | flops | bytes accessed | tf_op | source)
XLA Modules:
  0.0 78.8 jit_solution(17256895620223883456)
XLA Ops:
  0.6 0.0 copy-start
  0.6 1.6 %copy-done = bf16[2048,512]{1,0:T(8,128)(2,1)S(1)} copy-done((bf16[2048,512]{1,0:T(8,128)(2,1)S(1)}, bf16[2048,512]{1,0:T(8,128)(2,1)}, u32[]{:S(2)}) %copy-start) | copy-done | bytes 2097176
  2.2 0.0 copy-start.1
  2.2 0.9 %copy-done.1 = bf16[1,2,256,256]{3,2,1,0:T(8,128)(2,1)S(1)} copy-done((bf16[1,2,256,256]{3,2,1,0:T(8,128)(2,1)S(1)}, bf16[1,2,256,256]{3,2,1,0:T(8,128)(2,1)}, u32[]{:S(2)}) %copy-start.1) | copy-done | bytes 262168
  3.2 0.0 copy-start.2
  3.2 0.8 copy-done.2
  3.9 0.0 copy-start.3
  3.9 0.7 copy-done.3
  4.6 71.4 %selected_inverse.1 = (bf16[1,2048,512]{2,1,0:T(8,128)(2,1)S(1)}, bf16[1,512,512]{2,1,0:T(8,128)(2,1)S(1)}, bf16[1,2,256,256]{3,2,1,0:T(8,128)(2,1)S(1)}) custom-call(s32[1,2,8]{2,1,0:T(2,128)S(1)} %copy-done.3, s32[1,2,8]{2,1,0:T(2,128)S(1)} %copy-done.3, bf16[1,64,256]{2,1,0:T(8,128)(2,1)S(1)} %copy-done.2, bf16[8,256,512]{2,1,0:T(8,128)(2,1)S(1)} %bitcast.1, ...), custom_call_target="tpu_custom_call" | custom-call | tf_op jit(solution)/shard_map/selected_inverse/pallas_call | solution.py:300
  76.0 1.3 %copy.10 = bf16[1,2048,512]{2,1,0:T(8,128)(2,1)} copy(bf16[1,2048,512]{2,1,0:T(8,128)(2,1)S(1)} %get-tuple-element.6) | data formatting | bytes 4194304
  77.3 0.8 %copy.11 = bf16[1,512,512]{2,1,0:T(8,128)(2,1)} copy(bf16[1,512,512]{2,1,0:T(8,128)(2,1)S(1)} %get-tuple-element.7) | data formatting | bytes 1048576
  78.1 0.7 copy.12
Async XLA Ops:
  0.6 1.6 %copy-start = (bf16[2048,512]{1,0:T(8,128)(2,1)S(1)}, bf16[2048,512]{1,0:T(8,128)(2,1)}, u32[]{:S(2)}) copy-start(bf16[2048,512]{1,0:T(8,128)(2,1)} %param.4) | copy-start | bytes 6291460
  2.2 0.9 %copy-start.1 = (bf16[1,2,256,256]{3,2,1,0:T(8,128)(2,1)S(1)}, bf16[1,2,256,256]{3,2,1,0:T(8,128)(2,1)}, u32[]{:S(2)}) copy-start(bf16[1,2,256,256]{3,2,1,0:T(8,128)(2,1)} %dinv.1) | copy-start | bytes 786436
  3.2 0.8 copy-start.2
  3.9 0.7 copy-start.3

commit v2 on v0

v2 whole, which is shorter than its diff:
```python
import functools

import jax
import jax.numpy as jnp
from jax import lax
from jax.experimental import pallas as pl
from jax.experimental.pallas import tpu as pltpu
from jax.sharding import PartitionSpec as P

BLOCK = 256
ANCESTORS = 8
SUPERS = 2
TOP_BLOCKS = 28
SIDE = 4
PLANE = 16
QUARTER = 64
HALVES = 2
HALF = BLOCK // HALVES
SLOTS = SUPERS * ANCESTORS
MESH = pl.DeviceIdType.MESH
BF16 = jnp.bfloat16
F32 = jnp.float32
VMEM_LIMIT = 64 << 20

ROUTES = (
    ((("y", "z", "x"), 0, 32), (("x", "z", "y"), 32, 32)),
    ((("y", "z", "x"), 0, 16), (("z", "x", "y"), 16, 16), (("x", "y", "z"), 32, 32)),
)
HOPS = (2, 1, 3)
LINKS = 56


class Gather:
    def __init__(self, buf, dims, me, layer, routes, send, recv):
        self.buf, self.dims, self.me, self.layer, self.routes = buf, dims, me, layer, routes
        self.send, self.recv = send, recv
        self.count = 0
        self.sent, self.second, self.third = [], [], []

    def copies(self, route, full, axis, fixed=None):
        _, first, rows = route
        fixed = fixed or {}
        index = tuple(
            fixed[d] if d in fixed else pl.ds(0, SIDE) if d in full else self.me[d]
            for d in self.dims
        )
        part = self.buf.at[index + (pl.ds(first, rows),)]
        made = []
        for hop in HOPS:
            at = dict(self.me)
            at[axis] = (self.me[axis] + hop) % SIDE
            copy = pltpu.make_async_remote_copy(
                src_ref=part, dst_ref=part,
                send_sem=self.send.at[self.count], recv_sem=self.recv.at[self.count],
                device_id=(self.layer, at["x"], at["z"] * SIDE + at["y"]), device_id_type=MESH,
            )
            self.count += 1
            copy.start()
            made.append(copy)
        self.sent += made
        return made

    def start(self):
        self.first = [self.copies(route, (), route[0][0]) for route in self.routes]

    def after_first(self):
        for route, arriving in zip(self.routes, self.first):
            order = route[0]
            for copy in arriving:
                copy.wait_recv()
            self.second.append(self.copies(route, order[:1], order[1]))
        for route in self.routes:
            order = route[0]
            self.third += self.copies(route, order[:1], order[2])

    def after_second(self):
        for n, hop in enumerate(HOPS):
            for route, arriving in zip(self.routes, self.second):
                order = route[0]
                arriving[n].wait_recv()
                came_from = (self.me[order[1]] + SIDE - hop) % SIDE
                self.third += self.copies(route, order[:1], order[2], {order[1]: came_from})

    def finish(self):
        for copy in self.third:
            copy.wait_recv()

    def wait_sent(self):
        for copy in self.sent:
            copy.wait_send()


def kernel(
    anc_any, panel_any, g_any, dinv_any,
    tiles_out, diag_out,
    anc, dinv, panels, g_own, g_pick, panel_t, partial, partial_in, summed, staged, moved0, moved1, slots,
    sibling_slots0, sibling_slots1, sibling_diag, diag_send, tiles, diag, anc_in, anc_other,
    g_sem, in_sem, anc_send, anc_recv, anc_local,
    send1, recv1, send2, recv2, x_send, x_recv, c_send, c_recv, a_send, a_recv, d_send, d_recv, out_sem,
):
    layer = lax.axis_index("layer")
    x = lax.axis_index("prow")
    c = lax.axis_index("pcol")
    z = c // SIDE
    y = c % SIDE
    me = {"x": x, "y": y, "z": z}
    halves = range(HALVES)
    last = ANCESTORS - 1
    moved = (moved0, moved1)
    sibling_slots = (sibling_slots0, sibling_slots1)

    in_copies = [
        pltpu.make_async_copy(
            panel_any.at[0, :, pl.ds(h * HALF, HALF)], panels.at[h, x, z, y], in_sem.at[h]
        )
        for h in halves
    ]
    anc_load = pltpu.make_async_copy(anc_any, anc, in_sem.at[2])
    dinv_load = pltpu.make_async_copy(dinv_any, dinv, in_sem.at[3])
    g_load = pltpu.make_async_copy(g_any, g_own, g_sem)
    for copy in in_copies:
        copy.start()
    anc_load.start()
    g_load.start()
    dinv_load.start()

    barrier = pltpu.get_barrier_semaphore()

    def greet_plane(step, carry):
        pl.semaphore_signal(barrier, inc=1, device_id=(layer, x, (c + step) % PLANE), device_id_type=MESH)
        return carry

    def greet_line(step, carry):
        pl.semaphore_signal(barrier, inc=1, device_id=(layer, (x + step) % SIDE, c), device_id_type=MESH)
        return carry

    lax.fori_loop(1, PLANE, greet_plane, 0)
    lax.fori_loop(1, SIDE, greet_line, 0)
    pl.semaphore_signal(barrier, inc=1, device_id=(1 - layer, x, c), device_id_type=MESH)
    pl.semaphore_wait(barrier, PLANE - 1 + SIDE - 1 + 1)

    gather1 = [
        Gather(panels.at[h], ("x", "z", "y"), me, layer, ROUTES[h], send1.at[h], recv1.at[h])
        for h in halves
    ]
    gather2 = [
        Gather(slots.at[h], ("z", "y", "x"), me, layer, ROUTES[h], send2.at[h], recv2.at[h])
        for h in halves
    ]
    for copy in in_copies:
        copy.wait()
    gather1[0].start()
    sibling = (1 - layer, x, c)
    anc_copy = pltpu.make_async_remote_copy(
        src_ref=anc_any, dst_ref=anc_in, send_sem=anc_send, recv_sem=anc_recv,
        device_id=sibling, device_id_type=MESH,
    )
    anc_copy.start()
    anc_load.wait()
    g_load.wait()
    dinv_load.wait()

    def pick_blocks(k):
        def pick(p, carry):
            at = anc[0, k, p] - x * ANCESTORS
            here = jnp.logical_and(at >= 0, at < ANCESTORS)
            block = g_own[jnp.clip(at, 0, ANCESTORS - 1)]
            block = jnp.where(here, block, jnp.zeros_like(block))
            turned = block.T
            for b in range(2):
                for q in range(SIDE):
                    first = b * BLOCK + q * QUARTER
                    g_pick[k, p, q, b] = turned[first:first + QUARTER]
            return carry
        lax.fori_loop(0, ANCESTORS, pick, 0)

    def panel_tile(h, k, p):
        return panels[h, 2 * k + p // SIDE, p % SIDE].reshape(BLOCK, HALF)

    def multiply(h):
        for k in range(SUPERS):
            total = jnp.zeros((2 * BLOCK, HALF), F32)
            for p in range(ANCESTORS):
                total += jnp.dot(
                    g_pick[k, p].reshape(2 * BLOCK, BLOCK), panel_tile(h, k, p),
                    preferred_element_type=F32,
                )
            partial[h, :, k] = total.astype(BF16).reshape(SIDE, 2, QUARTER, HALF)

    x_copies = [[], []]

    def start_reduce(h):
        for hop in HOPS:
            to = (x + hop) % SIDE
            copy = pltpu.make_async_remote_copy(
                src_ref=partial.at[h, to], dst_ref=partial_in.at[h, hop - 1],
                send_sem=x_send.at[h, hop - 1], recv_sem=x_recv.at[h, hop - 1],
                device_id=(layer, to, c), device_id_type=MESH,
            )
            copy.start()
            x_copies[h].append(copy)

    def turn_panels(h):
        for k in range(SUPERS):
            for p in range(ANCESTORS):
                panel_t[k, p, h * HALF:(h + 1) * HALF, :] = panel_tile(h, k, p).T

    def to_slot(h, step):
        to = (c + step) % PLANE
        return pltpu.make_async_remote_copy(
            src_ref=staged.at[h, to], dst_ref=moved[h].at[c],
            send_sem=c_send.at[h, step], recv_sem=c_recv.at[h, step],
            device_id=(layer, x, to), device_id_type=MESH,
        )

    def each_slot(h, act):
        def step_of(step, carry):
            act(to_slot(h, step))
            return carry
        lax.fori_loop(1, PLANE, step_of, 0)

    def start_move(h):
        for copy in x_copies[h]:
            copy.wait_recv()
        total = partial[h, x].astype(F32)
        for hop in HOPS:
            total += partial_in[h, hop - 1].astype(F32)
        summed[h] = total.astype(BF16)
        for s in range(SLOTS):
            at = jnp.clip(anc[0, s // ANCESTORS, s % ANCESTORS] - 2 * c, 0, 1)
            staged[h, s] = summed[h, s // ANCESTORS, at]
        each_slot(h, lambda copy: copy.start())
        moved[h][c] = staged[h, c]

    def end_move(h):
        each_slot(h, lambda copy: copy.wait_recv())
        holder = anc[0, c // ANCESTORS, c % ANCESTORS] // 2
        slots[h, z, y, x] = moved[h][holder]

    def a_copy(h):
        return pltpu.make_async_remote_copy(
            src_ref=slots.at[h], dst_ref=sibling_slots[h], send_sem=a_send.at[h], recv_sem=a_recv.at[h],
            device_id=sibling, device_id_type=MESH,
        )

    def d_copy(h):
        return pltpu.make_async_remote_copy(
            src_ref=diag_send.at[h], dst_ref=sibling_diag.at[h], send_sem=d_send.at[h], recv_sem=d_recv.at[h],
            device_id=sibling, device_id_type=MESH,
        )

    def slot_tile(ref, s):
        return ref[s // SIDE, s % SIDE].reshape(BLOCK, HALF)

    def out_copy(k, first, count):
        return pltpu.make_async_copy(
            tiles.at[k, pl.ds(first, count)], tiles_out.at[k, pl.ds(first, count)],
            out_sem.at[k, first // last],
        )

    diag_store = pltpu.make_async_copy(diag, diag_out, out_sem.at[2, 0])

    pick_blocks(0)
    gather1[0].after_first()
    gather1[1].start()
    pick_blocks(1)
    gather1[0].after_second()
    gather1[1].after_first()
    gather1[0].finish()
    gather1[1].after_second()
    multiply(0)
    start_reduce(0)
    turn_panels(0)
    gather1[1].finish()
    multiply(1)
    start_reduce(1)
    start_move(0)
    turn_panels(1)
    start_move(1)
    end_move(0)
    gather2[0].start()
    anc_copy.wait_recv()
    to_smem = pltpu.make_async_copy(anc_in, anc_other, anc_local)
    to_smem.start()
    to_smem.wait()
    gather2[0].after_first()
    end_move(1)
    gather2[1].start()
    gather2[0].after_second()
    gather2[1].after_first()
    gather2[0].finish()

    @pl.when(layer == 0)
    def _():
        a_copy(0).start()

    gather2[1].after_second()

    @pl.when(layer == 0)
    def _():
        def half(h):
            for k in range(SUPERS):
                total = dinv[0, k, :, h * HALF:(h + 1) * HALF].astype(F32)
                for q in range(ANCESTORS):
                    total += jnp.dot(
                        panel_t[k, q], slot_tile(slots.at[h], k * ANCESTORS + q),
                        preferred_element_type=F32,
                    )
                diag_send[h, k] = total.astype(BF16)
                diag[0, k, :, h * HALF:(h + 1) * HALF] = total.astype(BF16)
            d_copy(h).start()
            for k in range(SUPERS):
                for q in range(ANCESTORS):
                    tiles[k, q, :, h * HALF:(h + 1) * HALF] = -slot_tile(slots.at[h], k * ANCESTORS + q)

        half(0)
        gather2[1].finish()
        a_copy(1).start()
        half(1)
        diag_store.start()
        for k in range(SUPERS):
            out_copy(k, 0, ANCESTORS).start()
        for h in halves:
            a_copy(h).wait_send()
            d_copy(h).wait_send()
        for k in range(SUPERS):
            out_copy(k, 0, ANCESTORS).wait()
        diag_store.wait()

    @pl.when(layer == 1)
    def _():
        parents, places = [], []
        for k in range(SUPERS):
            parent = jnp.clip(anc[0, k, last] - TOP_BLOCKS, 0, SUPERS - 1)
            found = []
            for q in range(last):
                at = jnp.int32(0)
                for j in range(ANCESTORS):
                    at = jnp.where(anc_other[0, parent, j] == anc[0, k, q], j, at)
                found.append(parent * ANCESTORS + at)
            parents.append(parent)
            places.append(found)

        def turned_half(h):
            sums = []
            for k in range(SUPERS):
                total = jnp.zeros((BLOCK, HALF), F32)
                for q in range(last):
                    total += jnp.dot(
                        panel_t[k, q], slot_tile(sibling_slots[h], places[k][q]),
                        preferred_element_type=F32,
                    )
                sums.append(total.T)
            return sums

        a_copy(0).wait_recv()
        turned0 = turned_half(0)
        gather2[1].finish()
        a_copy(1).wait_recv()
        turned1 = turned_half(1)
        edges = [
            jnp.concatenate([panel_tile(h, k, last) for h in halves], axis=1) for k in range(SUPERS)
        ]
        for k in range(SUPERS):
            for q in range(last):
                whole = jnp.concatenate(
                    [slot_tile(sibling_slots[h], places[k][q]) for h in halves], axis=1
                )
                new = jnp.dot(whole, edges[k], preferred_element_type=F32)
                for h in halves:
                    old = slot_tile(slots.at[h], k * ANCESTORS + q).astype(F32)
                    tiles[k, q, :, h * HALF:(h + 1) * HALF] = (
                        new[:, h * HALF:(h + 1) * HALF] - old
                    ).astype(BF16)
            out_copy(k, 0, last).start()
        for h in halves:
            d_copy(h).wait_recv()
        for k in range(SUPERS):
            above = jnp.concatenate([sibling_diag[h, parents[k]] for h in halves], axis=1)
            turned = jnp.concatenate([turned0[k], turned1[k]], axis=0)
            tiles[k, last] = (
                turned - jnp.dot(above, edges[k], preferred_element_type=F32)
            ).astype(BF16)
            tiles[k, ANCESTORS] = (
                turned - jnp.dot(above.T, edges[k], preferred_element_type=F32)
            ).astype(BF16)
            out_copy(k, last, 2).start()
            total = dinv[0, k].astype(F32)
            for q in range(ANCESTORS):
                total -= jnp.dot(panel_t[k, q], tiles[k, q], preferred_element_type=F32)
            diag[0, k] = total.astype(BF16)
        diag_store.start()
        for k in range(SUPERS):
            out_copy(k, 0, last).wait()
            out_copy(k, last, 2).wait()
        diag_store.wait()

    anc_copy.wait_send()
    for h in halves:
        gather1[h].wait_sent()
        gather2[h].wait_sent()
        for copy in x_copies[h]:
            copy.wait_send()
        each_slot(h, lambda copy: copy.wait_send())


def place(anc, tiles, diag, col_out, row_out, diag_out, zero, col_sem, row_sem, diag_sem):
    layer = lax.axis_index("layer")
    x = lax.axis_index("prow")
    c = lax.axis_index("pcol")
    zero[...] = jnp.zeros_like(zero)
    diag_copy = pltpu.make_async_copy(diag, diag_out, diag_sem)
    diag_copy.start()

    def put(out, sems, first, blocks, row_side, start):
        for k in range(SUPERS):
            for j in range(blocks):
                dst = out.at[0, pl.ds(j * BLOCK, BLOCK), pl.ds(k * BLOCK, BLOCK)]
                sem = sems.at[k, j]
                if not start:
                    pltpu.make_async_copy(zero, dst, sem).wait()
                    continue
                at = jnp.int32(0)
                hit = jnp.int32(0)
                for q in range(ANCESTORS):
                    same = anc[0, k, q] == first + j
                    at = jnp.where(same, q, at)
                    hit = jnp.where(same, 1, hit)
                if row_side:
                    turned = jnp.logical_and(layer == 1, at == ANCESTORS - 1)
                    at = jnp.where(turned, ANCESTORS, at)

                @pl.when(hit > 0)
                def _():
                    pltpu.make_async_copy(tiles.at[k, at], dst, sem).start()

                @pl.when(hit == 0)
                def _():
                    pltpu.make_async_copy(zero, dst, sem).start()

    for start in (True, False):
        put(col_out, col_sem, x * ANCESTORS, ANCESTORS, False, start)
        put(row_out, row_sem, c * 2, 2, True, start)
    diag_copy.wait()


def body(stored_inverse, lhat, diag_inverse, ancestors):
    rows, cols = stored_inverse.shape
    stored = stored_inverse.reshape(rows // BLOCK, BLOCK, cols)
    anywhere = pl.BlockSpec(memory_space=pl.ANY)
    smem = pl.BlockSpec(memory_space=pltpu.SMEM)
    dma = pltpu.SemaphoreType.DMA
    width = SUPERS * BLOCK
    piece = (HALVES, SIDE, SIDE, SIDE, QUARTER, HALF)
    tiles, diag = pl.pallas_call(
        kernel,
        out_shape=(
            jax.ShapeDtypeStruct((SUPERS, ANCESTORS + 1, BLOCK, BLOCK), BF16),
            jax.ShapeDtypeStruct(diag_inverse.shape, BF16),
        ),
        in_specs=[anywhere] * 4,
        out_specs=(anywhere, anywhere),
        scratch_shapes=[
            pltpu.SMEM(ancestors.shape, jnp.int32),
            pltpu.VMEM(diag_inverse.shape, BF16),
            pltpu.VMEM(piece, BF16),
            pltpu.VMEM((rows // BLOCK, BLOCK, cols), BF16),
            pltpu.VMEM((SUPERS, ANCESTORS, SIDE, 2, QUARTER, BLOCK), BF16),
            pltpu.VMEM((SUPERS, ANCESTORS, BLOCK, BLOCK), BF16),
            pltpu.VMEM((HALVES, SIDE, SUPERS, 2, QUARTER, HALF), BF16),
            pltpu.VMEM((HALVES, SIDE - 1, SUPERS, 2, QUARTER, HALF), BF16),
            pltpu.VMEM((HALVES, SUPERS, 2, QUARTER, HALF), BF16),
            pltpu.VMEM((HALVES, SLOTS, QUARTER, HALF), BF16),
            pltpu.VMEM((PLANE, QUARTER, HALF), BF16),
            pltpu.VMEM((PLANE, QUARTER, HALF), BF16),
            pltpu.VMEM(piece, BF16),
            pltpu.VMEM(piece[1:], BF16),
            pltpu.VMEM(piece[1:], BF16),
            pltpu.VMEM((HALVES, SUPERS, BLOCK, HALF), BF16),
            pltpu.VMEM((HALVES, SUPERS, BLOCK, HALF), BF16),
            pltpu.VMEM((SUPERS, ANCESTORS + 1, BLOCK, BLOCK), BF16),
            pltpu.VMEM(diag_inverse.shape, BF16),
            pltpu.VMEM(ancestors.shape, jnp.int32),
            pltpu.SMEM(ancestors.shape, jnp.int32),
            dma, dma((4,)), dma, dma, dma,
            dma((HALVES, LINKS)), dma((HALVES, LINKS)), dma((HALVES, LINKS)), dma((HALVES, LINKS)),
            dma((HALVES, 3)), dma((HALVES, 3)), dma((HALVES, PLANE)), dma((HALVES, PLANE)),
            dma((HALVES,)), dma((HALVES,)), dma((HALVES,)), dma((HALVES,)), dma((3, 2)),
        ],
        compiler_params=pltpu.CompilerParams(
            collective_id=0, has_side_effects=True, vmem_limit_bytes=VMEM_LIMIT
        ),
        name="selected_inverse",
    )(ancestors, lhat, stored, diag_inverse)
    return pl.pallas_call(
        place,
        out_shape=(
            jax.ShapeDtypeStruct((1, rows, width), BF16),
            jax.ShapeDtypeStruct((1, cols, width), BF16),
            jax.ShapeDtypeStruct(diag_inverse.shape, BF16),
        ),
        in_specs=[smem, anywhere, anywhere],
        out_specs=(anywhere, anywhere, anywhere),
        scratch_shapes=[
            pltpu.VMEM((BLOCK, BLOCK), BF16),
            dma((SUPERS, ANCESTORS)), dma((SUPERS, 2)), dma,
        ],
        compiler_params=pltpu.CompilerParams(vmem_limit_bytes=VMEM_LIMIT),
        name="placed_tiles",
    )(ancestors, tiles, diag)


def solution(mesh):
    return jax.shard_map(
        body,
        mesh=mesh,
        in_specs=(
            P("prow", "pcol"),
            P("layer", ("prow", "pcol"), None),
            P("layer", None, None, None),
            P("layer", None, None),
        ),
        out_specs=(
            P("layer", "prow", None),
            P("layer", "pcol", None),
            P("layer", None, None, None),
        ),
        check_vma=False,
    )
```

time: 672 us -> 111 us (0.17)
  waiting for transfers between devices: 548 us -> 0 us
  Pallas kernels: 0 us -> 110 us
  local copies, waits for them, and re-layouts: 54.5 us -> 0 us
  blocking collectives: 23.4 us -> 0 us
  matrix products: 16.9 us -> 0 us
  between operations: 14.4 us -> 0.64 us
  other arithmetic: 12.6 us -> 0 us
    psum x2 -> x0, waiting for transfers between devices: 232 us -> none  [body(): lax.psum(diag_part(panel_share, x_part, SUPERS), ('prow', 'pcol'))]
    all_gather x3 -> x0, waiting for transfers between devices: 160 us -> none  [the longest x2 89 us: body(): x_rows = lax.all_gather(x_part, 'pcol', axis=0, tiled=True)]
    unnamed x13 -> x0, waiting for transfers between devices: 152 us -> none
    pallas_call x0 -> x2, Pallas kernels: none -> 110 us  [the longest x1 68 us: body(): pl.pallas_call(kernel, out_shape=(jax.ShapeDtypeStruct((SUPERS, ANCESTORS...]
    unnamed x61 -> x0, local copies, waits for them, and re-layouts: 40.5 us -> none
    all_gather x2 -> x0, blocking collectives: 23.4 us -> none  [body(): y_cols = lax.all_gather(y_part, 'prow', axis=0, tiled=True)]
    dot_general x8 -> x0, matrix products: 16.9 us -> none  [the longest x2 5.87 us: place_panels(): jnp.einsum('kpm,kpxy->mxky', onehot, panel_tiles, preferred_element_type=...]
  transfers between devices with their start and end apart: 10 -> 0, of which waited for: 10 -> 0; matrix products, arithmetic and copies ran while one was open for 8% -> 0% of each run, Pallas kernels for 0% -> 0%
where the time goes in v2:
time: 111 us; the launch traced here: 110 us
  Pallas kernels  110 us (99%)
    pallas_call x1, Pallas kernels, body(): pl.pallas_call(kernel, out_shape=(jax.ShapeDtypeStruct((SUPERS, ANCESTORS...  68 us
    pallas_call x1, Pallas kernels, body(): pl.pallas_call(place, out_shape=(jax.ShapeDtypeStruct((1, rows, width), B...  41.7 us

profile of v2, /device:TPU:1, one launch (start us, length us, event | category | flops | bytes accessed | tf_op | source)
XLA Modules:
  0.0 110.3 jit_solution(13616983595402705708)
XLA Ops:
  0.6 68.0 %selected_inverse.1 = (bf16[2,9,256,256]{3,2,1,0:T(8,128)(2,1)}, bf16[1,2,256,256]{3,2,1,0:T(8,128)(2,1)}) custom-call(s32[1,2,8]{2,1,0:T(2,128)} %anc.1, bf16[1,64,256]{2,1,0:T(8,128)(2,1)} %panel_any.1, bf16[8,256,512]{2,1,0:T(8,128)(2,1)} %bitcast.1, bf16[1,2,256,256]{3,2,1,0:T(8,128)(2,1)} %dinv_any.1), custom_call_target="tpu_custom_call" | custom-call | tf_op jit(solution)/shard_map/selected_inverse/pallas_call | solution.py:455
  68.6 41.7 %placed_tiles.1 = (bf16[1,2048,512]{2,1,0:T(8,128)(2,1)}, bf16[1,512,512]{2,1,0:T(8,128)(2,1)}, bf16[1,2,256,256]{3,2,1,0:T(8,128)(2,1)}) custom-call(s32[1,2,8]{2,1,0:T(2,128)} %anc.1, bf16[2,9,256,256]{3,2,1,0:T(8,128)(2,1)} %get-tuple-element.5.tiles, bf16[1,2,256,256]{3,2,1,0:T(8,128)(2,1)} %get-tuple-element.6.diag), custom_call_target="tpu_custom_call" | custom-call | tf_op jit(solution)/shard_map/placed_tiles/pallas_call | solution.py:495

commit v3 on v2

--- a/solution.py
+++ b/solution.py
@@ -20,7 +20,7 @@
 MESH = pl.DeviceIdType.MESH
 BF16 = jnp.bfloat16
 F32 = jnp.float32
-VMEM_LIMIT = 64 << 20
+VMEM_LIMIT = 60 << 20
 
 ROUTES = (
     ((("y", "z", "x"), 0, 32), (("x", "z", "y"), 32, 32)),
@@ -448,6 +448,7 @@
     rows, cols = stored_inverse.shape
     stored = stored_inverse.reshape(rows // BLOCK, BLOCK, cols)
     anywhere = pl.BlockSpec(memory_space=pl.ANY)
+    vmem = pl.BlockSpec(memory_space=pltpu.VMEM)
     smem = pl.BlockSpec(memory_space=pltpu.SMEM)
     dma = pltpu.SemaphoreType.DMA
     width = SUPERS * BLOCK
@@ -455,11 +456,11 @@
     tiles, diag = pl.pallas_call(
         kernel,
         out_shape=(
-            jax.ShapeDtypeStruct((SUPERS, ANCESTORS + 1, BLOCK, BLOCK), BF16),
-            jax.ShapeDtypeStruct(diag_inverse.shape, BF16),
+            pltpu.VMEM((SUPERS, ANCESTORS + 1, BLOCK, BLOCK), BF16),
+            pltpu.VMEM(diag_inverse.shape, BF16),
         ),
         in_specs=[anywhere] * 4,
-        out_specs=(anywhere, anywhere),
+        out_specs=(vmem, vmem),
         scratch_shapes=[
             pltpu.SMEM(ancestors.shape, jnp.int32),
             pltpu.VMEM(diag_inverse.shape, BF16),
@@ -499,13 +500,13 @@
             jax.ShapeDtypeStruct((1, cols, width), BF16),
             jax.ShapeDtypeStruct(diag_inverse.shape, BF16),
         ),
-        in_specs=[smem, anywhere, anywhere],
+        in_specs=[smem, vmem, vmem],
         out_specs=(anywhere, anywhere, anywhere),
         scratch_shapes=[
             pltpu.VMEM((BLOCK, BLOCK), BF16),
             dma((SUPERS, ANCESTORS)), dma((SUPERS, 2)), dma,
         ],
-        compiler_params=pltpu.CompilerParams(vmem_limit_bytes=VMEM_LIMIT),
+        compiler_params=pltpu.CompilerParams(vmem_limit_bytes=VMEM_LIMIT // 8),
         name="placed_tiles",
     )(ancestors, tiles, diag)
 

time: 111 us -> 71.4 us (0.64)
  Pallas kernels: 110 us -> 70.7 us
    pallas_call x1, Pallas kernels: 41.7 us -> 2.31 us  [body(): pl.pallas_call(place, out_shape=(jax.ShapeDtypeStruct((1, rows, width), B...]
where the time goes in v3:
time: 71.4 us; the launch traced here: 71.3 us
  Pallas kernels  70.7 us (99%)
    pallas_call x1, Pallas kernels, body(): pl.pallas_call(kernel, out_shape=(pltpu.VMEM((SUPERS, ANCESTORS + 1, BLOC...  68.4 us
    pallas_call x1, Pallas kernels, body(): pl.pallas_call(place, out_shape=(jax.ShapeDtypeStruct((1, rows, width), B...  2.31 us

profile of v3, /device:TPU:1, one launch (start us, length us, event | category | flops | bytes accessed | tf_op | source)
XLA Modules:
  0.0 71.3 jit_solution(13934403521842381774)
XLA Ops:
  0.6 0.0 copy-start
  0.6 68.4 %selected_inverse.1 = (bf16[2,9,256,256]{3,2,1,0:T(8,128)(2,1)S(1)}, bf16[1,2,256,256]{3,2,1,0:T(8,128)(2,1)S(1)}) custom-call(s32[1,2,8]{2,1,0:T(2,128)} %anc.1, bf16[1,64,256]{2,1,0:T(8,128)(2,1)} %panel_any.1, bf16[8,256,512]{2,1,0:T(8,128)(2,1)} %bitcast.1, bf16[1,2,256,256]{3,2,1,0:T(8,128)(2,1)} %dinv_any.1), custom_call_target="tpu_custom_call" | custom-call | tf_op jit(solution)/shard_map/selected_inverse/pallas_call | solution.py:456
  69.0 0.0 copy-done
  69.0 2.3 %placed_tiles.1 = (bf16[1,2048,512]{2,1,0:T(8,128)(2,1)}, bf16[1,512,512]{2,1,0:T(8,128)(2,1)}, bf16[1,2,256,256]{3,2,1,0:T(8,128)(2,1)}) custom-call(s32[1,2,8]{2,1,0:T(2,128)S(1)} %copy-done, bf16[2,9,256,256]{3,2,1,0:T(8,128)(2,1)S(1)} %get-tuple-element.5.tiles, bf16[1,2,256,256]{3,2,1,0:T(8,128)(2,1)S(1)} %get-tuple-element.6.diag), custom_call_target="tpu_custom_call" | custom-call | tf_op jit(solution)/shard_map/placed_tiles/pallas_call | solution.py:496
Async XLA Ops:
  0.6 68.4 %copy-start = (s32[1,2,8]{2,1,0:T(2,128)S(1)}, s32[1,2,8]{2,1,0:T(2,128)}, u32[]{:S(2)}) copy-start(s32[1,2,8]{2,1,0:T(2,128)} %anc.1) | copy-start | bytes 196

commit v4 on v3

v4 whole, which is shorter than its diff:
```python
import jax
import jax.numpy as jnp
from jax import lax
from jax.experimental import pallas as pl
from jax.experimental.pallas import tpu as pltpu
from jax.sharding import PartitionSpec as P

BLOCK = 256
ANCESTORS = 8
SUPERS = 2
TOP_BLOCKS = 28
SIDE = 4
PLANE = 16
PIECES = 64
QUARTER = 64
SLOTS = SUPERS * ANCESTORS
LAST = ANCESTORS - 1
MESH = pl.DeviceIdType.MESH
BF16 = jnp.bfloat16
F32 = jnp.float32
VMEM_LIMIT = 60 << 20

ROUTES = (
    (("y", "z", "x"), (0, 48), (0, 128)),
    (("x", "z", "y"), (0, 48), (128, 128)),
    (("x", "y", "z"), (48, 16), (0, 256)),
)
HOPS = (2, 1, 3)
ARRIVALS = (1, 3, 2)
UNIT = 16 * 128
PIECE = QUARTER * BLOCK // UNIT


def units(route):
    return route[1][1] * route[2][1] // UNIT


class Gather:
    def __init__(self, buf, dims, me, layer, wait, send, first, second, third):
        self.buf, self.dims, self.me, self.layer, self.wait = buf, dims, me, layer, wait
        self.send, self.first, self.second, self.third = send, first, second, third

    def part(self, route, full, fixed=None):
        fixed = fixed or {}
        index = tuple(
            fixed[d] if d in fixed else pl.ds(0, SIDE) if d in full else self.me[d]
            for d in self.dims
        )
        return index + (pl.ds(*route[1]), pl.ds(*route[2]))

    def copies(self, route, full, axis, sem_of, fixed=None):
        part = self.buf.at[self.part(route, full, fixed)]
        for hop in HOPS:
            at = dict(self.me)
            at[axis] = (self.me[axis] + hop) % SIDE
            pltpu.make_async_remote_copy(
                src_ref=part, dst_ref=part, send_sem=self.send, recv_sem=sem_of(hop),
                device_id=(self.layer, at["x"], at["z"] * SIDE + at["y"]), device_id_type=MESH,
            ).start()

    def start(self):
        for r, route in enumerate(ROUTES):
            self.copies(route, (), route[0][0], lambda hop: self.first.at[r])

    def after_first(self):
        for r, route in enumerate(ROUTES):
            order = route[0]
            self.wait(self.first.at[r], 3 * units(route))
            self.copies(route, order[:1], order[1], lambda hop: self.second.at[r, hop - 1])
        for r, route in enumerate(ROUTES):
            order = route[0]
            self.copies(route, order[:1], order[2], lambda hop: self.third.at[r, hop - 1])

    def after_second(self):
        for hop in ARRIVALS:
            for r, route in enumerate(ROUTES):
                order = route[0]
                self.wait(self.second.at[r, hop - 1], SIDE * units(route))
                came_from = (self.me[order[1]] + SIDE - hop) % SIDE
                self.copies(
                    route, order[:1], order[2], lambda to: self.third.at[r, to - 1], {order[1]: came_from}
                )

    def own_planes(self, act):
        for route in ROUTES:
            act(self.part(route, route[0][:2]))

    def finish(self, act=None):
        for hop in ARRIVALS:
            for r, route in enumerate(ROUTES):
                order = route[0]
                self.wait(self.third.at[r, hop - 1], PLANE * units(route))
                if act is not None:
                    came_from = (self.me[order[2]] + SIDE - hop) % SIDE
                    act(self.part(route, order[:2], {order[2]: came_from}))

    def wait_sent(self):
        self.wait(self.send, (PIECES - 1) * PIECE)


def kernel(
    anc_any, panel_any, g_any, dinv_any,
    tiles, diag,
    anc, dinv, panels, g_own, g_pick, panel_t, partial, partial_in, summed, staged, moved, slots,
    other_slots, other_panel_t, other_edges, diag_now, corner_send, corner_in, anc_in, anc_other, measure,
    in_sem, anc_sem,
    send1, first1, second1, third1, send2, first2, second2, third2,
    x_send, x_recv, c_send, c_recv, a_send, a_recv, m_send, m_recv, e_send, e_recv,
):
    layer = lax.axis_index("layer")
    x = lax.axis_index("prow")
    c = lax.axis_index("pcol")
    z = c // SIDE
    y = c % SIDE
    me = {"x": x, "y": y, "z": z}
    sibling = (1 - layer, x, c)

    def wait(sem, count):
        ref = measure.at[pl.ds(0, count)]
        pltpu.make_async_copy(ref, ref, sem).wait()

    def to_sibling(src, dst, send, recv):
        return pltpu.make_async_remote_copy(
            src_ref=src, dst_ref=dst, send_sem=send, recv_sem=recv, device_id=sibling, device_id_type=MESH
        )

    panel_load = pltpu.make_async_copy(panel_any, panels.at[x, z, pl.ds(y, 1)], in_sem.at[0])
    anc_load = pltpu.make_async_copy(anc_any, anc, in_sem.at[1])
    dinv_load = pltpu.make_async_copy(dinv_any, dinv, in_sem.at[2])
    g_load = pltpu.make_async_copy(g_any, g_own, in_sem.at[3])
    panel_load.start()
    anc_load.start()
    g_load.start()
    dinv_load.start()

    barrier = pltpu.get_barrier_semaphore()

    def greet_plane(step, carry):
        pl.semaphore_signal(barrier, inc=1, device_id=(layer, x, (c + step) % PLANE), device_id_type=MESH)
        return carry

    def greet_line(step, carry):
        pl.semaphore_signal(barrier, inc=1, device_id=(layer, (x + step) % SIDE, c), device_id_type=MESH)
        return carry

    lax.fori_loop(1, PLANE, greet_plane, 0)
    lax.fori_loop(1, SIDE, greet_line, 0)
    pl.semaphore_signal(barrier, inc=1, device_id=sibling, device_id_type=MESH)
    pl.semaphore_wait(barrier, PLANE - 1 + SIDE - 1 + 1)

    gather1 = Gather(panels, ("x", "z", "y"), me, layer, wait, send1, first1, second1, third1)
    gather2 = Gather(slots, ("z", "y", "x"), me, layer, wait, send2, first2, second2, third2)
    panel_load.wait()
    gather1.start()
    anc_copy = to_sibling(anc_any, anc_in, anc_sem.at[0], anc_sem.at[1])
    anc_copy.start()
    anc_load.wait()
    dinv_load.wait()
    g_load.wait()

    def pick_blocks(k):
        def pick(p, carry):
            at = anc[0, k, p] - x * ANCESTORS
            here = jnp.logical_and(at >= 0, at < ANCESTORS)
            block = g_own[jnp.clip(at, 0, ANCESTORS - 1)]
            block = jnp.where(here, block, jnp.zeros_like(block))
            turned = block.T
            for b in range(2):
                for q in range(SIDE):
                    first = b * BLOCK + q * QUARTER
                    g_pick[k, p, q, b] = turned[first:first + QUARTER]
            return carry
        lax.fori_loop(0, ANCESTORS, pick, 0)

    def tile_of(ref, s):
        return ref[s // SIDE, s % SIDE].reshape(BLOCK, BLOCK)

    def multiply(k):
        total = jnp.zeros((2 * BLOCK, BLOCK), F32)
        for p in range(ANCESTORS):
            total += jnp.dot(
                g_pick[k, p].reshape(2 * BLOCK, BLOCK), tile_of(panels, k * ANCESTORS + p),
                preferred_element_type=F32,
            )
        partial[k] = total.astype(BF16).reshape(SIDE, 2, QUARTER, BLOCK)

    def start_reduce(k):
        for hop in HOPS:
            to = (x + hop) % SIDE
            pltpu.make_async_remote_copy(
                src_ref=partial.at[k, to], dst_ref=partial_in.at[k, hop - 1],
                send_sem=x_send, recv_sem=x_recv.at[k],
                device_id=(layer, to, c), device_id_type=MESH,
            ).start()

    def turn_panels():
        for k in range(SUPERS):
            def turn(p, carry):
                s = k * ANCESTORS + p
                panel_t[k, p] = tile_of(panels, s).T
                return carry
            lax.fori_loop(0, ANCESTORS, turn, 0)

    def start_move(k):
        wait(x_recv.at[k], 3 * 2 * PIECE)
        total = partial[k, x].astype(F32)
        for hop in HOPS:
            total += partial_in[k, hop - 1].astype(F32)
        summed[k] = total.astype(BF16)
        for q in range(ANCESTORS):
            staged[k * ANCESTORS + q] = summed[k, jnp.clip(anc[0, k, q] - 2 * c, 0, 1)]

        def send(step, carry):
            to = k * ANCESTORS + (c + step) % ANCESTORS

            @pl.when(to != c)
            def _():
                pltpu.make_async_remote_copy(
                    src_ref=staged.at[to], dst_ref=moved.at[c], send_sem=c_send, recv_sem=c_recv,
                    device_id=(layer, x, to), device_id_type=MESH,
                ).start()
            return carry
        lax.fori_loop(0, ANCESTORS, send, 0)

    def end_move():
        moved[c] = staged[c]
        wait(c_recv, (PLANE - 1) * PIECE)
        holder = anc[0, c // ANCESTORS, c % ANCESTORS] // 2
        slots[z, y, x] = moved[holder]

    gather1.after_first()
    pick_blocks(0)
    gather1.after_second()
    pick_blocks(1)
    gather1.finish()
    multiply(0)
    start_reduce(0)
    multiply(1)
    start_reduce(1)
    turn_panels()

    @pl.when(layer == 1)
    def _():
        to_sibling(panel_t, other_panel_t, m_send.at[0], m_recv.at[0]).start()
        for k in range(SUPERS):
            to_sibling(
                panels.at[2 * k + 1, SIDE - 1], other_edges.at[k], m_send.at[k + 1], m_recv.at[k + 1]
            ).start()

    anc_copy.wait_recv()
    to_smem = pltpu.make_async_copy(anc_in, anc_other, in_sem.at[1])
    to_smem.start()
    to_smem.wait()
    start_move(0)
    start_move(1)
    end_move()
    gather2.start()

    def find_parents(above, below):
        parents, places = [], []
        for k in range(SUPERS):
            parent = jnp.clip(below[0, k, LAST] - TOP_BLOCKS, 0, SUPERS - 1)
            found = []
            for q in range(LAST):
                at = jnp.int32(0)
                for j in range(ANCESTORS):
                    at = jnp.where(above[0, parent, j] == below[0, k, q], j, at)
                found.append(parent * ANCESTORS + at)
            parents.append(parent)
            places.append(found)
        return parents, places

    gather2.after_first()
    gather2.after_second()

    def pass_on(part):
        to_sibling(slots.at[part], other_slots.at[part], a_send, a_recv).start()

    def corner_copy(k):
        return to_sibling(corner_send.at[k], corner_in.at[k], e_send.at[k], e_recv.at[k])

    def matrix(a, b):
        return jnp.dot(a, b, preferred_element_type=F32)

    @pl.when(layer == 0)
    def _():
        parents, places = find_parents(anc, anc_other)
        gather2.own_planes(pass_on)
        gather2.finish(pass_on)
        to_sibling(panel_t, other_panel_t, m_send.at[0], m_recv.at[0]).wait_recv()
        for k in range(SUPERS):
            to_sibling(
                panels.at[2 * k + 1, SIDE - 1], other_edges.at[k], m_send.at[k + 1], m_recv.at[k + 1]
            ).wait_recv()
        for k in range(SUPERS):
            total = dinv[0, k].astype(F32)
            for q in range(ANCESTORS):
                total += matrix(panel_t[k, q], tile_of(slots, k * ANCESTORS + q))
            diag[0, k] = total.astype(BF16)
            diag_now[k] = total.astype(BF16)
        for k in range(SUPERS):
            total = jnp.zeros((BLOCK, BLOCK), F32)
            for q in range(LAST):
                total += matrix(other_panel_t[k, q], tile_of(slots, places[k][q]))
            above = diag_now[parents[k]]
            edge = other_edges[k].reshape(BLOCK, BLOCK)
            turned = total.T
            corner_send[k, 0] = (turned - matrix(above, edge)).astype(BF16)
            corner_send[k, 1] = (turned - matrix(above.T, edge)).astype(BF16)
            corner_send[k, 2] = total.astype(BF16)
            corner_copy(k).start()
        for k in range(SUPERS):
            for q in range(ANCESTORS):
                tiles[k, q] = -tile_of(slots, k * ANCESTORS + q)
        wait(a_send, PIECES * PIECE)
        for k in range(SUPERS):
            corner_copy(k).wait_send()

    @pl.when(layer == 1)
    def _():
        parents, places = find_parents(anc_other, anc)
        gather2.finish()
        sums = []
        for k in range(SUPERS):
            total = dinv[0, k].astype(F32)
            for q in range(LAST):
                total += matrix(panel_t[k, q], tile_of(slots, k * ANCESTORS + q))
            sums.append(total)
        wait(a_recv, PIECES * PIECE)
        for k in range(SUPERS):
            edge = tile_of(panels, k * ANCESTORS + LAST)
            for q in range(LAST):
                new = matrix(tile_of(other_slots, places[k][q]), edge)
                tiles[k, q] = (new - tile_of(slots, k * ANCESTORS + q).astype(F32)).astype(BF16)
        for k in range(SUPERS):
            corner_copy(k).wait_recv()
            corner = corner_in[k, 0]
            tiles[k, LAST] = corner
            tiles[k, ANCESTORS] = corner_in[k, 1]
            edge = tile_of(panels, k * ANCESTORS + LAST)
            total = sums[k] - matrix(corner_in[k, 2], edge) - matrix(panel_t[k, LAST], corner)
            diag[0, k] = total.astype(BF16)
        to_sibling(panel_t, other_panel_t, m_send.at[0], m_recv.at[0]).wait_send()
        for k in range(SUPERS):
            to_sibling(
                panels.at[2 * k + 1, SIDE - 1], other_edges.at[k], m_send.at[k + 1], m_recv.at[k + 1]
            ).wait_send()

    anc_copy.wait_send()
    gather1.wait_sent()
    gather2.wait_sent()
    wait(x_send, SUPERS * 3 * 2 * PIECE)
    wait(c_send, (PLANE - 1) * PIECE)


def place(anc, tiles, diag, col_out, row_out, diag_out, zero, col_sem, row_sem, diag_sem):
    layer = lax.axis_index("layer")
    x = lax.axis_index("prow")
    c = lax.axis_index("pcol")
    zero[...] = jnp.zeros_like(zero)
    diag_copy = pltpu.make_async_copy(diag, diag_out, diag_sem)
    diag_copy.start()

    def put(out, sems, first, blocks, row_side, start):
        for k in range(SUPERS):
            for j in range(blocks):
                dst = out.at[0, pl.ds(j * BLOCK, BLOCK), pl.ds(k * BLOCK, BLOCK)]
                sem = sems.at[k, j]
                if not start:
                    pltpu.make_async_copy(zero, dst, sem).wait()
                    continue
                at = jnp.int32(0)
                hit = jnp.int32(0)
                for q in range(ANCESTORS):
                    same = anc[0, k, q] == first + j
                    at = jnp.where(same, q, at)
                    hit = jnp.where(same, 1, hit)
                if row_side:
                    turned = jnp.logical_and(layer == 1, at == ANCESTORS - 1)
                    at = jnp.where(turned, ANCESTORS, at)

                @pl.when(hit > 0)
                def _():
                    pltpu.make_async_copy(tiles.at[k, at], dst, sem).start()

                @pl.when(hit == 0)
                def _():
                    pltpu.make_async_copy(zero, dst, sem).start()

    for start in (True, False):
        put(col_out, col_sem, x * ANCESTORS, ANCESTORS, False, start)
        put(row_out, row_sem, c * 2, 2, True, start)
    diag_copy.wait()


def body(stored_inverse, lhat, diag_inverse, ancestors):
    rows, cols = stored_inverse.shape
    stored = stored_inverse.reshape(rows // BLOCK, BLOCK, cols)
    anywhere = pl.BlockSpec(memory_space=pl.ANY)
    vmem = pl.BlockSpec(memory_space=pltpu.VMEM)
    smem = pl.BlockSpec(memory_space=pltpu.SMEM)
    dma = pltpu.SemaphoreType.DMA
    width = SUPERS * BLOCK
    pieces = (SIDE, SIDE, SIDE, QUARTER, BLOCK)
    square = (SUPERS, ANCESTORS, BLOCK, BLOCK)
    gather_sems = [dma, dma((3,)), dma((3, 3)), dma((3, 3))]
    tiles, diag = pl.pallas_call(
        kernel,
        out_shape=(
            pltpu.VMEM((SUPERS, ANCESTORS + 1, BLOCK, BLOCK), BF16),
            pltpu.VMEM(diag_inverse.shape, BF16),
        ),
        in_specs=[anywhere] * 4,
        out_specs=(vmem, vmem),
        scratch_shapes=[
            pltpu.SMEM(ancestors.shape, jnp.int32),
            pltpu.VMEM(diag_inverse.shape, BF16),
            pltpu.VMEM(pieces, BF16),
            pltpu.VMEM((rows // BLOCK, BLOCK, cols), BF16),
            pltpu.VMEM((SUPERS, ANCESTORS, SIDE, 2, QUARTER, BLOCK), BF16),
            pltpu.VMEM(square, BF16),
            pltpu.VMEM((SUPERS, SIDE, 2, QUARTER, BLOCK), BF16),
            pltpu.VMEM((SUPERS, SIDE - 1, 2, QUARTER, BLOCK), BF16),
            pltpu.VMEM((SUPERS, 2, QUARTER, BLOCK), BF16),
            pltpu.VMEM((SLOTS, QUARTER, BLOCK), BF16),
            pltpu.VMEM((PLANE, QUARTER, BLOCK), BF16),
            pltpu.VMEM(pieces, BF16),
            pltpu.VMEM(pieces, BF16),
            pltpu.VMEM(square, BF16),
            pltpu.VMEM((SUPERS, SIDE, QUARTER, BLOCK), BF16),
            pltpu.VMEM((SUPERS, BLOCK, BLOCK), BF16),
            pltpu.VMEM((SUPERS, 3, BLOCK, BLOCK), BF16),
            pltpu.VMEM((SUPERS, 3, BLOCK, BLOCK), BF16),
            pltpu.VMEM(ancestors.shape, jnp.int32),
            pltpu.SMEM(ancestors.shape, jnp.int32),
            pltpu.VMEM((PIECES * PIECE, 16, 128), BF16),
            dma((4,)), dma((2,)), *gather_sems, *gather_sems,
            dma, dma((SUPERS,)), dma, dma, dma, dma, dma((3,)), dma((3,)), dma((SUPERS,)), dma((SUPERS,)),
        ],
        compiler_params=pltpu.CompilerParams(
            collective_id=0, has_side_effects=True, vmem_limit_bytes=VMEM_LIMIT
        ),
        name="selected_inverse",
    )(ancestors, lhat, stored, diag_inverse)
    return pl.pallas_call(
        place,
        out_shape=(
            jax.ShapeDtypeStruct((1, rows, width), BF16),
            jax.ShapeDtypeStruct((1, cols, width), BF16),
            jax.ShapeDtypeStruct(diag_inverse.shape, BF16),
        ),
        in_specs=[smem, vmem, vmem],
        out_specs=(anywhere, anywhere, anywhere),
        scratch_shapes=[
            pltpu.VMEM((BLOCK, BLOCK), BF16),
            dma((SUPERS, ANCESTORS)), dma((SUPERS, 2)), dma,
        ],
        compiler_params=pltpu.CompilerParams(vmem_limit_bytes=VMEM_LIMIT // 8),
        name="placed_tiles",
    )(ancestors, tiles, diag)


def solution(mesh):
    return jax.shard_map(
        body,
        mesh=mesh,
        in_specs=(
            P("prow", "pcol"),
            P("layer", ("prow", "pcol"), None),
            P("layer", None, None, None),
            P("layer", None, None),
        ),
        out_specs=(
            P("layer", "prow", None),
            P("layer", "pcol", None),
            P("layer", None, None, None),
        ),
        check_vma=False,
    )
```

time: 71.4 us -> 62.5 us (0.88)
  Pallas kernels: 70.7 us -> 61.8 us
    pallas_call x1, Pallas kernels: 68.4 us -> 59.5 us  [body(): pl.pallas_call(kernel, out_shape=(pltpu.VMEM((SUPERS, ANCESTORS + 1, BLOC...]
where the time goes in v4:
time: 62.5 us; the launch traced here: 62.4 us
  Pallas kernels  61.8 us (99%)
  between operations  0.65 us (1%)
    pallas_call x1, Pallas kernels, body(): pl.pallas_call(kernel, out_shape=(pltpu.VMEM((SUPERS, ANCESTORS + 1, BLOC...  59.5 us
    pallas_call x1, Pallas kernels, body(): pl.pallas_call(place, out_shape=(jax.ShapeDtypeStruct((1, rows, width), B...  2.31 us

profile of v4, /device:TPU:1, one launch (start us, length us, event | category | flops | bytes accessed | tf_op | source)
XLA Modules:
  0.0 62.4 jit_solution(15106103025861172265)
XLA Ops:
  0.6 0.0 copy-start
  0.6 59.5 %selected_inverse.1 = (bf16[2,9,256,256]{3,2,1,0:T(8,128)(2,1)S(1)}, bf16[1,2,256,256]{3,2,1,0:T(8,128)(2,1)S(1)}) custom-call(s32[1,2,8]{2,1,0:T(2,128)} %anc.1, bf16[1,64,256]{2,1,0:T(8,128)(2,1)} %panel_any.1, bf16[8,256,512]{2,1,0:T(8,128)(2,1)} %bitcast.1, bf16[1,2,256,256]{3,2,1,0:T(8,128)(2,1)} %dinv_any.1), custom_call_target="tpu_custom_call" | custom-call | tf_op jit(solution)/shard_map/selected_inverse/pallas_call | solution.py:407
  60.1 0.0 copy-done
  60.1 2.3 %placed_tiles.1 = (bf16[1,2048,512]{2,1,0:T(8,128)(2,1)}, bf16[1,512,512]{2,1,0:T(8,128)(2,1)}, bf16[1,2,256,256]{3,2,1,0:T(8,128)(2,1)}) custom-call(s32[1,2,8]{2,1,0:T(2,128)S(1)} %copy-done, bf16[2,9,256,256]{3,2,1,0:T(8,128)(2,1)S(1)} %get-tuple-element.5.tiles, bf16[1,2,256,256]{3,2,1,0:T(8,128)(2,1)S(1)} %get-tuple-element.6.diag), custom_call_target="tpu_custom_call" | custom-call | tf_op jit(solution)/shard_map/placed_tiles/pallas_call | solution.py:445
Async XLA Ops:
  0.6 59.5 %copy-start = (s32[1,2,8]{2,1,0:T(2,128)S(1)}, s32[1,2,8]{2,1,0:T(2,128)}, u32[]{:S(2)}) copy-start(s32[1,2,8]{2,1,0:T(2,128)} %anc.1) | copy-start | bytes 196

commit v5 on v4

--- a/solution.py
+++ b/solution.py
@@ -20,19 +20,13 @@
 F32 = jnp.float32
 VMEM_LIMIT = 60 << 20
 
-ROUTES = (
-    (("y", "z", "x"), (0, 48), (0, 128)),
-    (("x", "z", "y"), (0, 48), (128, 128)),
-    (("x", "y", "z"), (48, 16), (0, 256)),
-)
 HOPS = (2, 1, 3)
 ARRIVALS = (1, 3, 2)
+NEXT = {"x": "y", "y": "z", "z": "x"}
+WAY = {"x": 0, "y": 1, "z": 2}
+PAIRS = sorted(((h, g) for h in ARRIVALS for g in ARRIVALS), key=lambda pair: pair.count(2))
 UNIT = 16 * 128
 PIECE = QUARTER * BLOCK // UNIT
-
-
-def units(route):
-    return route[1][1] * route[2][1] // UNIT
 
 
 class Gather:
@@ -40,59 +34,63 @@
         self.buf, self.dims, self.me, self.layer, self.wait = buf, dims, me, layer, wait
         self.send, self.first, self.second, self.third = send, first, second, third
 
-    def part(self, route, full, fixed=None):
-        fixed = fixed or {}
-        index = tuple(
-            fixed[d] if d in fixed else pl.ds(0, SIDE) if d in full else self.me[d]
-            for d in self.dims
-        )
-        return index + (pl.ds(*route[1]), pl.ds(*route[2]))
-
-    def copies(self, route, full, axis, sem_of, fixed=None):
-        part = self.buf.at[self.part(route, full, fixed)]
+    def moved(self, **hops):
+        at = dict(self.me)
+        for axis, hop in hops.items():
+            at[axis] = (self.me[axis] + SIDE + hop) % SIDE
+        return at
+
+    def index(self, at):
+        return tuple(at[d] for d in self.dims)
+
+    def pass_on(self, at, axis, hop, sem):
+        piece = self.buf.at[self.index(at)]
+        to = self.moved(**{axis: hop})
+        pltpu.make_async_remote_copy(
+            src_ref=piece, dst_ref=piece, send_sem=self.send, recv_sem=sem,
+            device_id=(self.layer, to["x"], to["z"] * SIDE + to["y"]), device_id_type=MESH,
+        ).start()
+
+    def start(self):
         for hop in HOPS:
-            at = dict(self.me)
-            at[axis] = (self.me[axis] + hop) % SIDE
-            pltpu.make_async_remote_copy(
-                src_ref=part, dst_ref=part, send_sem=self.send, recv_sem=sem_of(hop),
-                device_id=(self.layer, at["x"], at["z"] * SIDE + at["y"]), device_id_type=MESH,
-            ).start()
-
-    def start(self):
-        for r, route in enumerate(ROUTES):
-            self.copies(route, (), route[0][0], lambda hop: self.first.at[r])
+            for n, axis in enumerate("xyz"):
+                self.pass_on(self.me, axis, hop, self.first.at[n, hop - 1])
 
     def after_first(self):
-        for r, route in enumerate(ROUTES):
-            order = route[0]
-            self.wait(self.first.at[r], 3 * units(route))
-            self.copies(route, order[:1], order[1], lambda hop: self.second.at[r, hop - 1])
-        for r, route in enumerate(ROUTES):
-            order = route[0]
-            self.copies(route, order[:1], order[2], lambda hop: self.third.at[r, hop - 1])
+        for hop in ARRIVALS:
+            for n, axis in enumerate("xyz"):
+                self.wait(self.first.at[n, hop - 1], PIECE)
+                source = self.moved(**{axis: -hop})
+                for to in HOPS:
+                    self.pass_on(source, NEXT[axis], to, self.second.at[n, hop - 1, to - 1])
 
     def after_second(self):
+        for pair, (hop, then) in enumerate(PAIRS):
+            for n, axis in enumerate("xyz"):
+                self.wait(self.second.at[n, hop - 1, then - 1], PIECE)
+                by = NEXT[axis]
+                source = self.moved(**{axis: -hop, by: -then})
+                last = next(f for f in ARRIVALS if (hop + then + f) % 3 == WAY[axis])
+                self.pass_on(source, NEXT[by], last, self.third.at[pair])
+
+    def nearer(self):
+        i, j, k = self.dims
+        yield (self.me[i],)
         for hop in ARRIVALS:
-            for r, route in enumerate(ROUTES):
-                order = route[0]
-                self.wait(self.second.at[r, hop - 1], SIDE * units(route))
-                came_from = (self.me[order[1]] + SIDE - hop) % SIDE
-                self.copies(
-                    route, order[:1], order[2], lambda to: self.third.at[r, to - 1], {order[1]: came_from}
-                )
-
-    def own_planes(self, act):
-        for route in ROUTES:
-            act(self.part(route, route[0][:2]))
+            yield self.moved(**{i: hop})[i], self.me[j]
+        for hop in ARRIVALS:
+            for then in ARRIVALS:
+                at = self.moved(**{i: hop, j: then})
+                yield self.index(at)
 
     def finish(self, act=None):
-        for hop in ARRIVALS:
-            for r, route in enumerate(ROUTES):
-                order = route[0]
-                self.wait(self.third.at[r, hop - 1], PLANE * units(route))
-                if act is not None:
-                    came_from = (self.me[order[2]] + SIDE - hop) % SIDE
-                    act(self.part(route, order[:2], {order[2]: came_from}))
+        for pair, (hop, then) in enumerate(PAIRS):
+            self.wait(self.third.at[pair], 3 * PIECE)
+            if act is not None:
+                for axis in "xyz":
+                    by = NEXT[axis]
+                    last = next(f for f in ARRIVALS if (hop + then + f) % 3 == WAY[axis])
+                    act(self.index(self.moved(**{axis: -hop, by: -then, NEXT[by]: -last})))
 
     def wait_sent(self):
         self.wait(self.send, (PIECES - 1) * PIECE)
@@ -102,10 +100,10 @@
     anc_any, panel_any, g_any, dinv_any,
     tiles, diag,
     anc, dinv, panels, g_own, g_pick, panel_t, partial, partial_in, summed, staged, moved, slots,
-    other_slots, other_panel_t, other_edges, diag_now, corner_send, corner_in, anc_in, anc_other, measure,
+    other_slots, diag_now, diag_in, anc_in, anc_other, measure,
     in_sem, anc_sem,
     send1, first1, second1, third1, send2, first2, second2, third2,
-    x_send, x_recv, c_send, c_recv, a_send, a_recv, m_send, m_recv, e_send, e_recv,
+    x_send, x_recv, c_send, c_recv, a_send, a_recv, d_send, d_recv,
 ):
     layer = lax.axis_index("layer")
     x = lax.axis_index("prow")
@@ -239,14 +237,6 @@
     start_reduce(1)
     turn_panels()
 
-    @pl.when(layer == 1)
-    def _():
-        to_sibling(panel_t, other_panel_t, m_send.at[0], m_recv.at[0]).start()
-        for k in range(SUPERS):
-            to_sibling(
-                panels.at[2 * k + 1, SIDE - 1], other_edges.at[k], m_send.at[k + 1], m_recv.at[k + 1]
-            ).start()
-
     anc_copy.wait_recv()
     to_smem = pltpu.make_async_copy(anc_in, anc_other, in_sem.at[1])
     to_smem.start()
@@ -256,19 +246,17 @@
     end_move()
     gather2.start()
 
-    def find_parents(above, below):
-        parents, places = [], []
-        for k in range(SUPERS):
-            parent = jnp.clip(below[0, k, LAST] - TOP_BLOCKS, 0, SUPERS - 1)
-            found = []
-            for q in range(LAST):
-                at = jnp.int32(0)
-                for j in range(ANCESTORS):
-                    at = jnp.where(above[0, parent, j] == below[0, k, q], j, at)
-                found.append(parent * ANCESTORS + at)
-            parents.append(parent)
-            places.append(found)
-        return parents, places
+    parents, places = [], []
+    for k in range(SUPERS):
+        parent = jnp.clip(anc[0, k, LAST] - TOP_BLOCKS, 0, SUPERS - 1)
+        found = []
+        for q in range(LAST):
+            at = jnp.int32(0)
+            for j in range(ANCESTORS):
+                at = jnp.where(anc_other[0, parent, j] == anc[0, k, q], j, at)
+            found.append(parent * ANCESTORS + at)
+        parents.append(parent)
+        places.append(found)
 
     gather2.after_first()
     gather2.after_second()
@@ -276,75 +264,58 @@
     def pass_on(part):
         to_sibling(slots.at[part], other_slots.at[part], a_send, a_recv).start()
 
-    def corner_copy(k):
-        return to_sibling(corner_send.at[k], corner_in.at[k], e_send.at[k], e_recv.at[k])
+    d_copy = to_sibling(diag_now, diag_in, d_send, d_recv)
 
     def matrix(a, b):
         return jnp.dot(a, b, preferred_element_type=F32)
 
     @pl.when(layer == 0)
     def _():
-        parents, places = find_parents(anc, anc_other)
-        gather2.own_planes(pass_on)
+        for part in gather2.nearer():
+            pass_on(part)
         gather2.finish(pass_on)
-        to_sibling(panel_t, other_panel_t, m_send.at[0], m_recv.at[0]).wait_recv()
-        for k in range(SUPERS):
-            to_sibling(
-                panels.at[2 * k + 1, SIDE - 1], other_edges.at[k], m_send.at[k + 1], m_recv.at[k + 1]
-            ).wait_recv()
         for k in range(SUPERS):
             total = dinv[0, k].astype(F32)
             for q in range(ANCESTORS):
                 total += matrix(panel_t[k, q], tile_of(slots, k * ANCESTORS + q))
-            diag[0, k] = total.astype(BF16)
             diag_now[k] = total.astype(BF16)
-        for k in range(SUPERS):
-            total = jnp.zeros((BLOCK, BLOCK), F32)
-            for q in range(LAST):
-                total += matrix(other_panel_t[k, q], tile_of(slots, places[k][q]))
-            above = diag_now[parents[k]]
-            edge = other_edges[k].reshape(BLOCK, BLOCK)
-            turned = total.T
-            corner_send[k, 0] = (turned - matrix(above, edge)).astype(BF16)
-            corner_send[k, 1] = (turned - matrix(above.T, edge)).astype(BF16)
-            corner_send[k, 2] = total.astype(BF16)
-            corner_copy(k).start()
-        for k in range(SUPERS):
+        d_copy.start()
+        for k in range(SUPERS):
+            diag[0, k] = diag_now[k]
             for q in range(ANCESTORS):
                 tiles[k, q] = -tile_of(slots, k * ANCESTORS + q)
         wait(a_send, PIECES * PIECE)
-        for k in range(SUPERS):
-            corner_copy(k).wait_send()
+        d_copy.wait_send()
 
     @pl.when(layer == 1)
     def _():
-        parents, places = find_parents(anc_other, anc)
         gather2.finish()
-        sums = []
+        sums, edges = [], []
         for k in range(SUPERS):
             total = dinv[0, k].astype(F32)
             for q in range(LAST):
                 total += matrix(panel_t[k, q], tile_of(slots, k * ANCESTORS + q))
             sums.append(total)
+            edges.append(tile_of(panels, k * ANCESTORS + LAST))
         wait(a_recv, PIECES * PIECE)
-        for k in range(SUPERS):
-            edge = tile_of(panels, k * ANCESTORS + LAST)
+        crossed = []
+        for k in range(SUPERS):
+            total = jnp.zeros((BLOCK, BLOCK), F32)
             for q in range(LAST):
-                new = matrix(tile_of(other_slots, places[k][q]), edge)
-                tiles[k, q] = (new - tile_of(slots, k * ANCESTORS + q).astype(F32)).astype(BF16)
-        for k in range(SUPERS):
-            corner_copy(k).wait_recv()
-            corner = corner_in[k, 0]
+                tile = tile_of(other_slots, places[k][q])
+                total += matrix(panel_t[k, q], tile)
+                old = tile_of(slots, k * ANCESTORS + q).astype(F32)
+                tiles[k, q] = (matrix(tile, edges[k]) - old).astype(BF16)
+            crossed.append(total)
+        d_copy.wait_recv()
+        for k in range(SUPERS):
+            above = diag_in[parents[k]]
+            turned = crossed[k].T
+            corner = (turned - matrix(above, edges[k])).astype(BF16)
             tiles[k, LAST] = corner
-            tiles[k, ANCESTORS] = corner_in[k, 1]
-            edge = tile_of(panels, k * ANCESTORS + LAST)
-            total = sums[k] - matrix(corner_in[k, 2], edge) - matrix(panel_t[k, LAST], corner)
-            diag[0, k] = total.astype(BF16)
-        to_sibling(panel_t, other_panel_t, m_send.at[0], m_recv.at[0]).wait_send()
-        for k in range(SUPERS):
-            to_sibling(
-                panels.at[2 * k + 1, SIDE - 1], other_edges.at[k], m_send.at[k + 1], m_recv.at[k + 1]
-            ).wait_send()
+            tiles[k, ANCESTORS] = (turned - matrix(above.T, edges[k])).astype(BF16)
+            total = sums[k] - matrix(crossed[k].astype(BF16), edges[k])
+            diag[0, k] = (total - matrix(panel_t[k, LAST], corner)).astype(BF16)
 
     anc_copy.wait_send()
     gather1.wait_sent()
@@ -402,8 +373,7 @@
     dma = pltpu.SemaphoreType.DMA
     width = SUPERS * BLOCK
     pieces = (SIDE, SIDE, SIDE, QUARTER, BLOCK)
-    square = (SUPERS, ANCESTORS, BLOCK, BLOCK)
-    gather_sems = [dma, dma((3,)), dma((3, 3)), dma((3, 3))]
+    gather_sems = [dma, dma((3, 3)), dma((3, 3, 3)), dma((len(PAIRS),))]
     tiles, diag = pl.pallas_call(
         kernel,
         out_shape=(
@@ -418,7 +388,7 @@
             pltpu.VMEM(pieces, BF16),
             pltpu.VMEM((rows // BLOCK, BLOCK, cols), BF16),
             pltpu.VMEM((SUPERS, ANCESTORS, SIDE, 2, QUARTER, BLOCK), BF16),
-            pltpu.VMEM(square, BF16),
+            pltpu.VMEM((SUPERS, ANCESTORS, BLOCK, BLOCK), BF16),
             pltpu.VMEM((SUPERS, SIDE, 2, QUARTER, BLOCK), BF16),
             pltpu.VMEM((SUPERS, SIDE - 1, 2, QUARTER, BLOCK), BF16),
             pltpu.VMEM((SUPERS, 2, QUARTER, BLOCK), BF16),
@@ -426,16 +396,13 @@
             pltpu.VMEM((PLANE, QUARTER, BLOCK), BF16),
             pltpu.VMEM(pieces, BF16),
             pltpu.VMEM(pieces, BF16),
-            pltpu.VMEM(square, BF16),
-            pltpu.VMEM((SUPERS, SIDE, QUARTER, BLOCK), BF16),
             pltpu.VMEM((SUPERS, BLOCK, BLOCK), BF16),
-            pltpu.VMEM((SUPERS, 3, BLOCK, BLOCK), BF16),
-            pltpu.VMEM((SUPERS, 3, BLOCK, BLOCK), BF16),
+            pltpu.VMEM((SUPERS, BLOCK, BLOCK), BF16),
             pltpu.VMEM(ancestors.shape, jnp.int32),
             pltpu.SMEM(ancestors.shape, jnp.int32),
             pltpu.VMEM((PIECES * PIECE, 16, 128), BF16),
             dma((4,)), dma((2,)), *gather_sems, *gather_sems,
-            dma, dma((SUPERS,)), dma, dma, dma, dma, dma((3,)), dma((3,)), dma((SUPERS,)), dma((SUPERS,)),
+            dma, dma((SUPERS,)), dma, dma, dma, dma, dma, dma,
         ],
         compiler_params=pltpu.CompilerParams(
             collective_id=0, has_side_effects=True, vmem_limit_bytes=VMEM_LIMIT

time: 62.5 us -> 58.2 us (0.931)
  Pallas kernels: 61.8 us -> 57.4 us
    pallas_call x1, Pallas kernels: 59.5 us -> 55.1 us  [body(): pl.pallas_call(kernel, out_shape=(pltpu.VMEM((SUPERS, ANCESTORS + 1, BLOC...]
where the time goes in v5:
time: 58.2 us; the launch traced here: 58.1 us
  Pallas kernels  57.4 us (99%)
  between operations  0.65 us (1%)
    pallas_call x1, Pallas kernels, body(): pl.pallas_call(kernel, out_shape=(pltpu.VMEM((SUPERS, ANCESTORS + 1, BLOC...  55.1 us
    pallas_call x1, Pallas kernels, body(): pl.pallas_call(place, out_shape=(jax.ShapeDtypeStruct((1, rows, width), B...  2.31 us

profile of v5, /device:TPU:1, one launch (start us, length us, event | category | flops | bytes accessed | tf_op | source)
XLA Modules:
  0.0 58.1 jit_solution(9146767004350793304)
XLA Ops:
  0.6 0.0 copy-start
  0.6 55.1 %selected_inverse.1 = (bf16[2,9,256,256]{3,2,1,0:T(8,128)(2,1)S(1)}, bf16[1,2,256,256]{3,2,1,0:T(8,128)(2,1)S(1)}) custom-call(s32[1,2,8]{2,1,0:T(2,128)} %anc.1, bf16[1,64,256]{2,1,0:T(8,128)(2,1)} %panel_any.1, bf16[8,256,512]{2,1,0:T(8,128)(2,1)} %bitcast.1, bf16[1,2,256,256]{3,2,1,0:T(8,128)(2,1)} %dinv_any.1), custom_call_target="tpu_custom_call" | custom-call | tf_op jit(solution)/shard_map/selected_inverse/pallas_call | solution.py:377
  55.8 0.0 copy-done
  55.8 2.3 %placed_tiles.1 = (bf16[1,2048,512]{2,1,0:T(8,128)(2,1)}, bf16[1,512,512]{2,1,0:T(8,128)(2,1)}, bf16[1,2,256,256]{3,2,1,0:T(8,128)(2,1)}) custom-call(s32[1,2,8]{2,1,0:T(2,128)S(1)} %copy-done, bf16[2,9,256,256]{3,2,1,0:T(8,128)(2,1)S(1)} %get-tuple-element.5.tiles, bf16[1,2,256,256]{3,2,1,0:T(8,128)(2,1)S(1)} %get-tuple-element.6.diag), custom_call_target="tpu_custom_call" | custom-call | tf_op jit(solution)/shard_map/placed_tiles/pallas_call | solution.py:412
Async XLA Ops:
  0.6 55.1 %copy-start = (s32[1,2,8]{2,1,0:T(2,128)S(1)}, s32[1,2,8]{2,1,0:T(2,128)}, u32[]{:S(2)}) copy-start(s32[1,2,8]{2,1,0:T(2,128)} %anc.1) | copy-start | bytes 196

commit v6 on v5

--- a/solution.py
+++ b/solution.py
@@ -98,11 +98,11 @@
 
 def kernel(
     anc_any, panel_any, g_any, dinv_any,
-    tiles, diag,
-    anc, dinv, panels, g_own, g_pick, panel_t, partial, partial_in, summed, staged, moved, slots,
+    tiles, diag, anc,
+    dinv, panels, g_own, g_pick, panel_t, partial, partial_in, summed, staged, moved, slots,
     other_slots, diag_now, diag_in, anc_in, anc_other, measure,
     in_sem, anc_sem,
-    send1, first1, second1, third1, send2, first2, second2, third2,
+    send1, first1, second1, third1, send2, third2,
     x_send, x_recv, c_send, c_recv, a_send, a_recv, d_send, d_recv,
 ):
     layer = lax.axis_index("layer")
@@ -122,6 +122,12 @@
             src_ref=src, dst_ref=dst, send_sem=send, recv_sem=recv, device_id=sibling, device_id_type=MESH
         )
 
+    barrier = pltpu.get_barrier_semaphore()
+    greeted = [(layer, (x + step) % SIDE, c) for step in range(1, SIDE)]
+    greeted += [(layer, x, (c + step) % PLANE) for step in range(1, PLANE)]
+    greeted.append(sibling)
+    for device in greeted:
+        pl.semaphore_signal(barrier, inc=1, device_id=device, device_id_type=MESH)
     panel_load = pltpu.make_async_copy(panel_any, panels.at[x, z, pl.ds(y, 1)], in_sem.at[0])
     anc_load = pltpu.make_async_copy(anc_any, anc, in_sem.at[1])
     dinv_load = pltpu.make_async_copy(dinv_any, dinv, in_sem.at[2])
@@ -131,23 +137,10 @@
     g_load.start()
     dinv_load.start()
 
-    barrier = pltpu.get_barrier_semaphore()
-
-    def greet_plane(step, carry):
-        pl.semaphore_signal(barrier, inc=1, device_id=(layer, x, (c + step) % PLANE), device_id_type=MESH)
-        return carry
-
-    def greet_line(step, carry):
-        pl.semaphore_signal(barrier, inc=1, device_id=(layer, (x + step) % SIDE, c), device_id_type=MESH)
-        return carry
-
-    lax.fori_loop(1, PLANE, greet_plane, 0)
-    lax.fori_loop(1, SIDE, greet_line, 0)
-    pl.semaphore_signal(barrier, inc=1, device_id=sibling, device_id_type=MESH)
-    pl.semaphore_wait(barrier, PLANE - 1 + SIDE - 1 + 1)
+    pl.semaphore_wait(barrier, len(greeted))
 
     gather1 = Gather(panels, ("x", "z", "y"), me, layer, wait, send1, first1, second1, third1)
-    gather2 = Gather(slots, ("z", "y", "x"), me, layer, wait, send2, first2, second2, third2)
+    gather2 = Gather(slots, ("z", "y", "x"), me, layer, wait, send2, first1, second1, third2)
     panel_load.wait()
     gather1.start()
     anc_copy = to_sibling(anc_any, anc_in, anc_sem.at[0], anc_sem.at[1])
@@ -374,16 +367,16 @@
     width = SUPERS * BLOCK
     pieces = (SIDE, SIDE, SIDE, QUARTER, BLOCK)
     gather_sems = [dma, dma((3, 3)), dma((3, 3, 3)), dma((len(PAIRS),))]
-    tiles, diag = pl.pallas_call(
+    tiles, diag, lists = pl.pallas_call(
         kernel,
         out_shape=(
             pltpu.VMEM((SUPERS, ANCESTORS + 1, BLOCK, BLOCK), BF16),
             pltpu.VMEM(diag_inverse.shape, BF16),
+            pltpu.SMEM(ancestors.shape, jnp.int32),
         ),
         in_specs=[anywhere] * 4,
-        out_specs=(vmem, vmem),
+        out_specs=(vmem, vmem, smem),
         scratch_shapes=[
-            pltpu.SMEM(ancestors.shape, jnp.int32),
             pltpu.VMEM(diag_inverse.shape, BF16),
             pltpu.VMEM(pieces, BF16),
             pltpu.VMEM((rows // BLOCK, BLOCK, cols), BF16),
@@ -401,7 +394,7 @@
             pltpu.VMEM(ancestors.shape, jnp.int32),
             pltpu.SMEM(ancestors.shape, jnp.int32),
             pltpu.VMEM((PIECES * PIECE, 16, 128), BF16),
-            dma((4,)), dma((2,)), *gather_sems, *gather_sems,
+            dma((4,)), dma((2,)), *gather_sems, dma, dma((len(PAIRS),)),
             dma, dma((SUPERS,)), dma, dma, dma, dma, dma, dma,
         ],
         compiler_params=pltpu.CompilerParams(
@@ -424,7 +417,7 @@
         ],
         compiler_params=pltpu.CompilerParams(vmem_limit_bytes=VMEM_LIMIT // 8),
         name="placed_tiles",
-    )(ancestors, tiles, diag)
+    )(lists, tiles, diag)
 
 
 def solution(mesh):

time: 58.2 us -> 57.5 us (0.988)
  Pallas kernels: 57.4 us -> 56.7 us
where the time goes in v6:
time: 57.5 us; the launch traced here: 57.4 us
  Pallas kernels  56.7 us (99%)
  between operations  0.64 us (1%)
    pallas_call x1, Pallas kernels, body(): pl.pallas_call(kernel, out_shape=(pltpu.VMEM((SUPERS, ANCESTORS + 1, BLOC...  55 us
    pallas_call x1, Pallas kernels, body(): pl.pallas_call(place, out_shape=(jax.ShapeDtypeStruct((1, rows, width), B...  1.76 us

profile of v6, /device:TPU:1, one launch (start us, length us, event | category | flops | bytes accessed | tf_op | source)
XLA Modules:
  0.0 57.4 jit_solution(5653192376863035649)
XLA Ops:
  0.6 55.0 %selected_inverse.1 = (bf16[2,9,256,256]{3,2,1,0:T(8,128)(2,1)S(1)}, bf16[1,2,256,256]{3,2,1,0:T(8,128)(2,1)S(1)}, s32[1,2,8]{2,1,0:T(2,128)S(4)}) custom-call(s32[1,2,8]{2,1,0:T(2,128)} %anc_any.1, bf16[1,64,256]{2,1,0:T(8,128)(2,1)} %panel_any.1, bf16[8,256,512]{2,1,0:T(8,128)(2,1)} %bitcast.1, bf16[1,2,256,256]{3,2,1,0:T(8,128)(2,1)} %dinv_any.1), custom_call_target="tpu_custom_call" | custom-call | tf_op jit(solution)/shard_map/selected_inverse/pallas_call | solution.py:370
  55.6 1.8 %placed_tiles.1 = (bf16[1,2048,512]{2,1,0:T(8,128)(2,1)}, bf16[1,512,512]{2,1,0:T(8,128)(2,1)}, bf16[1,2,256,256]{3,2,1,0:T(8,128)(2,1)}) custom-call(s32[1,2,8]{2,1,0:T(2,128)S(4)} %get-tuple-element.6.anc, bf16[2,9,256,256]{3,2,1,0:T(8,128)(2,1)S(1)} %get-tuple-element.7.tiles, bf16[1,2,256,256]{3,2,1,0:T(8,128)(2,1)S(1)} %get-tuple-element.8.diag), custom_call_target="tpu_custom_call" | custom-call | tf_op jit(solution)/shard_map/placed_tiles/pallas_call | solution.py:405

commit v7 on v6

--- a/solution.py
+++ b/solution.py
@@ -65,32 +65,16 @@
                     self.pass_on(source, NEXT[axis], to, self.second.at[n, hop - 1, to - 1])
 
     def after_second(self):
-        for pair, (hop, then) in enumerate(PAIRS):
+        for hop, then in PAIRS:
             for n, axis in enumerate("xyz"):
                 self.wait(self.second.at[n, hop - 1, then - 1], PIECE)
                 by = NEXT[axis]
                 source = self.moved(**{axis: -hop, by: -then})
                 last = next(f for f in ARRIVALS if (hop + then + f) % 3 == WAY[axis])
-                self.pass_on(source, NEXT[by], last, self.third.at[pair])
-
-    def nearer(self):
-        i, j, k = self.dims
-        yield (self.me[i],)
-        for hop in ARRIVALS:
-            yield self.moved(**{i: hop})[i], self.me[j]
-        for hop in ARRIVALS:
-            for then in ARRIVALS:
-                at = self.moved(**{i: hop, j: then})
-                yield self.index(at)
-
-    def finish(self, act=None):
-        for pair, (hop, then) in enumerate(PAIRS):
-            self.wait(self.third.at[pair], 3 * PIECE)
-            if act is not None:
-                for axis in "xyz":
-                    by = NEXT[axis]
-                    last = next(f for f in ARRIVALS if (hop + then + f) % 3 == WAY[axis])
-                    act(self.index(self.moved(**{axis: -hop, by: -then, NEXT[by]: -last})))
+                self.pass_on(source, NEXT[by], last, self.third)
+
+    def finish(self):
+        self.wait(self.third, 27 * PIECE)
 
     def wait_sent(self):
         self.wait(self.send, (PIECES - 1) * PIECE)
@@ -100,10 +84,10 @@
     anc_any, panel_any, g_any, dinv_any,
     tiles, diag, anc,
     dinv, panels, g_own, g_pick, panel_t, partial, partial_in, summed, staged, moved, slots,
-    other_slots, diag_now, diag_in, anc_in, anc_other, measure,
+    other_panel_t, other_dinv, other_piece, anc_in, anc_other, measure,
     in_sem, anc_sem,
     send1, first1, second1, third1, send2, third2,
-    x_send, x_recv, c_send, c_recv, a_send, a_recv, d_send, d_recv,
+    x_send, x_recv, c_send, c_recv, a_send, a_recv, m_send, m_recv, d_send, d_recv,
 ):
     layer = lax.axis_index("layer")
     x = lax.axis_index("prow")
@@ -149,9 +133,21 @@
     dinv_load.wait()
     g_load.wait()
 
+    def parent_of(k):
+        return jnp.clip(anc[0, k, LAST] - TOP_BLOCKS, 0, SUPERS - 1)
+
+    def own_super(k):
+        child = jnp.where(parent_of(0) == k, 0, 1)
+        return jnp.where(layer == 0, k, child)
+
+    def slot_block(k, q):
+        return jnp.where(layer == 0, anc[0, k, q], anc_other[0, k, q])
+
     def pick_blocks(k):
+        own = own_super(k)
+
         def pick(p, carry):
-            at = anc[0, k, p] - x * ANCESTORS
+            at = anc[0, own, p] - x * ANCESTORS
             here = jnp.logical_and(at >= 0, at < ANCESTORS)
             block = g_own[jnp.clip(at, 0, ANCESTORS - 1)]
             block = jnp.where(here, block, jnp.zeros_like(block))
@@ -167,10 +163,11 @@
         return ref[s // SIDE, s % SIDE].reshape(BLOCK, BLOCK)
 
     def multiply(k):
+        own = own_super(k)
         total = jnp.zeros((2 * BLOCK, BLOCK), F32)
         for p in range(ANCESTORS):
             total += jnp.dot(
-                g_pick[k, p].reshape(2 * BLOCK, BLOCK), tile_of(panels, k * ANCESTORS + p),
+                g_pick[k, p].reshape(2 * BLOCK, BLOCK), tile_of(panels, own * ANCESTORS + p),
                 preferred_element_type=F32,
             )
         partial[k] = total.astype(BF16).reshape(SIDE, 2, QUARTER, BLOCK)
@@ -199,7 +196,7 @@
             total += partial_in[k, hop - 1].astype(F32)
         summed[k] = total.astype(BF16)
         for q in range(ANCESTORS):
-            staged[k * ANCESTORS + q] = summed[k, jnp.clip(anc[0, k, q] - 2 * c, 0, 1)]
+            staged[k * ANCESTORS + q] = summed[k, jnp.clip(slot_block(k, q) - 2 * c, 0, 1)]
 
         def send(step, carry):
             to = k * ANCESTORS + (c + step) % ANCESTORS
@@ -216,8 +213,24 @@
     def end_move():
         moved[c] = staged[c]
         wait(c_recv, (PLANE - 1) * PIECE)
-        holder = anc[0, c // ANCESTORS, c % ANCESTORS] // 2
-        slots[z, y, x] = moved[holder]
+        piece = moved[slot_block(c // ANCESTORS, c % ANCESTORS) // 2]
+        passed = to_sibling(slots.at[z, y, x], other_piece, a_send, a_recv)
+
+        @pl.when(layer == 0)
+        def _():
+            slots[z, y, x] = piece
+            passed.start()
+
+        @pl.when(layer == 1)
+        def _():
+            passed.wait_recv()
+            edge = tile_of(panels, own_super(c // ANCESTORS) * ANCESTORS + LAST)
+            new = jnp.dot(other_piece[...], edge, preferred_element_type=F32)
+            slots[z, y, x] = (new - piece.astype(F32)).astype(BF16)
+        return passed
+
+    m_copy = to_sibling(panel_t, other_panel_t, m_send, m_recv)
+    d_copy = to_sibling(dinv, other_dinv, d_send, d_recv)
 
     gather1.after_first()
     pick_blocks(0)
@@ -230,18 +243,23 @@
     start_reduce(1)
     turn_panels()
 
+    @pl.when(layer == 0)
+    def _():
+        m_copy.start()
+        d_copy.start()
+
     anc_copy.wait_recv()
     to_smem = pltpu.make_async_copy(anc_in, anc_other, in_sem.at[1])
     to_smem.start()
     to_smem.wait()
     start_move(0)
     start_move(1)
-    end_move()
+    passed = end_move()
     gather2.start()
 
     parents, places = [], []
     for k in range(SUPERS):
-        parent = jnp.clip(anc[0, k, LAST] - TOP_BLOCKS, 0, SUPERS - 1)
+        parent = parent_of(k)
         found = []
         for q in range(LAST):
             at = jnp.int32(0)
@@ -254,60 +272,46 @@
     gather2.after_first()
     gather2.after_second()
 
-    def pass_on(part):
-        to_sibling(slots.at[part], other_slots.at[part], a_send, a_recv).start()
-
-    d_copy = to_sibling(diag_now, diag_in, d_send, d_recv)
-
     def matrix(a, b):
         return jnp.dot(a, b, preferred_element_type=F32)
 
     @pl.when(layer == 0)
     def _():
-        for part in gather2.nearer():
-            pass_on(part)
-        gather2.finish(pass_on)
+        gather2.finish()
         for k in range(SUPERS):
             total = dinv[0, k].astype(F32)
             for q in range(ANCESTORS):
-                total += matrix(panel_t[k, q], tile_of(slots, k * ANCESTORS + q))
-            diag_now[k] = total.astype(BF16)
-        d_copy.start()
-        for k in range(SUPERS):
-            diag[0, k] = diag_now[k]
-            for q in range(ANCESTORS):
-                tiles[k, q] = -tile_of(slots, k * ANCESTORS + q)
-        wait(a_send, PIECES * PIECE)
+                tile = tile_of(slots, k * ANCESTORS + q)
+                total += matrix(panel_t[k, q], tile)
+                tiles[k, q] = -tile
+            diag[0, k] = total.astype(BF16)
+        passed.wait_send()
+        m_copy.wait_send()
         d_copy.wait_send()
 
     @pl.when(layer == 1)
     def _():
+        m_copy.wait_recv()
+        d_copy.wait_recv()
+        crossed, turned = [], []
+        for k in range(SUPERS):
+            edge = tile_of(panels, k * ANCESTORS + LAST)
+            above = other_dinv[0, parents[k]]
+            crossed.append(matrix(above, edge))
+            turned.append(matrix(above.T, edge))
         gather2.finish()
-        sums, edges = [], []
         for k in range(SUPERS):
+            total = jnp.zeros((BLOCK, BLOCK), F32)
+            for p in range(ANCESTORS):
+                total += matrix(other_panel_t[parents[k], p], tile_of(slots, parents[k] * ANCESTORS + p))
+            corner = (-total - crossed[k]).astype(BF16)
+            tiles[k, LAST] = corner
+            tiles[k, ANCESTORS] = (-total - turned[k]).astype(BF16)
             total = dinv[0, k].astype(F32)
             for q in range(LAST):
-                total += matrix(panel_t[k, q], tile_of(slots, k * ANCESTORS + q))
-            sums.append(total)
-            edges.append(tile_of(panels, k * ANCESTORS + LAST))
-        wait(a_recv, PIECES * PIECE)
-        crossed = []
-        for k in range(SUPERS):
-            total = jnp.zeros((BLOCK, BLOCK), F32)
-            for q in range(LAST):
-                tile = tile_of(other_slots, places[k][q])
-                total += matrix(panel_t[k, q], tile)
-                old = tile_of(slots, k * ANCESTORS + q).astype(F32)
-                tiles[k, q] = (matrix(tile, edges[k]) - old).astype(BF16)
-            crossed.append(total)
-        d_copy.wait_recv()
-        for k in range(SUPERS):
-            above = diag_in[parents[k]]
-            turned = crossed[k].T
-            corner = (turned - matrix(above, edges[k])).astype(BF16)
-            tiles[k, LAST] = corner
-            tiles[k, ANCESTORS] = (turned - matrix(above.T, edges[k])).astype(BF16)
-            total = sums[k] - matrix(crossed[k].astype(BF16), edges[k])
+                tile = tile_of(slots, places[k][q])
+                total -= matrix(panel_t[k, q], tile)
+                tiles[k, q] = tile
             diag[0, k] = (total - matrix(panel_t[k, LAST], corner)).astype(BF16)
 
     anc_copy.wait_send()
@@ -366,7 +370,7 @@
     dma = pltpu.SemaphoreType.DMA
     width = SUPERS * BLOCK
     pieces = (SIDE, SIDE, SIDE, QUARTER, BLOCK)
-    gather_sems = [dma, dma((3, 3)), dma((3, 3, 3)), dma((len(PAIRS),))]
+    gather_sems = [dma, dma((3, 3)), dma((3, 3, 3)), dma]
     tiles, diag, lists = pl.pallas_call(
         kernel,
         out_shape=(
@@ -388,14 +392,14 @@
             pltpu.VMEM((SLOTS, QUARTER, BLOCK), BF16),
             pltpu.VMEM((PLANE, QUARTER, BLOCK), BF16),
             pltpu.VMEM(pieces, BF16),
-            pltpu.VMEM(pieces, BF16),
-            pltpu.VMEM((SUPERS, BLOCK, BLOCK), BF16),
-            pltpu.VMEM((SUPERS, BLOCK, BLOCK), BF16),
+            pltpu.VMEM((SUPERS, ANCESTORS, BLOCK, BLOCK), BF16),
+            pltpu.VMEM(diag_inverse.shape, BF16),
+            pltpu.VMEM((QUARTER, BLOCK), BF16),
             pltpu.VMEM(ancestors.shape, jnp.int32),
             pltpu.SMEM(ancestors.shape, jnp.int32),
             pltpu.VMEM((PIECES * PIECE, 16, 128), BF16),
-            dma((4,)), dma((2,)), *gather_sems, dma, dma((len(PAIRS),)),
-            dma, dma((SUPERS,)), dma, dma, dma, dma, dma, dma,
+            dma((4,)), dma((2,)), *gather_sems, dma, dma,
+            dma, dma((SUPERS,)), dma, dma, dma, dma, dma, dma, dma, dma,
         ],
         compiler_params=pltpu.CompilerParams(
             collective_id=0, has_side_effects=True, vmem_limit_bytes=VMEM_LIMIT

time: 57.5 us -> 56.5 us (0.983)
  Pallas kernels: 56.7 us -> 55.8 us
    pallas_call x1, Pallas kernels: 55 us -> 54 us  [body(): pl.pallas_call(kernel, out_shape=(pltpu.VMEM((SUPERS, ANCESTORS + 1, BLOC...]
where the time goes in v7:
time: 56.5 us; the launch traced here: 56.4 us
  Pallas kernels  55.8 us (99%)
  between operations  0.64 us (1%)
    pallas_call x1, Pallas kernels, body(): pl.pallas_call(kernel, out_shape=(pltpu.VMEM((SUPERS, ANCESTORS + 1, BLOC...  54 us
    pallas_call x1, Pallas kernels, body(): pl.pallas_call(place, out_shape=(jax.ShapeDtypeStruct((1, rows, width), B...  1.76 us

profile of v7, /device:TPU:1, one launch (start us, length us, event | category | flops | bytes accessed | tf_op | source)
XLA Modules:
  0.0 56.4 jit_solution(4178293461408082675)
XLA Ops:
  0.6 54.0 %selected_inverse.1 = (bf16[2,9,256,256]{3,2,1,0:T(8,128)(2,1)S(1)}, bf16[1,2,256,256]{3,2,1,0:T(8,128)(2,1)S(1)}, s32[1,2,8]{2,1,0:T(2,128)S(4)}) custom-call(s32[1,2,8]{2,1,0:T(2,128)} %anc_any.1, bf16[1,64,256]{2,1,0:T(8,128)(2,1)} %panel_any.1, bf16[8,256,512]{2,1,0:T(8,128)(2,1)} %bitcast.1, bf16[1,2,256,256]{3,2,1,0:T(8,128)(2,1)} %dinv_any.1), custom_call_target="tpu_custom_call" | custom-call | tf_op jit(solution)/shard_map/selected_inverse/pallas_call | solution.py:374
  54.6 1.8 %placed_tiles.1 = (bf16[1,2048,512]{2,1,0:T(8,128)(2,1)}, bf16[1,512,512]{2,1,0:T(8,128)(2,1)}, bf16[1,2,256,256]{3,2,1,0:T(8,128)(2,1)}) custom-call(s32[1,2,8]{2,1,0:T(2,128)S(4)} %get-tuple-element.6.anc, bf16[2,9,256,256]{3,2,1,0:T(8,128)(2,1)S(1)} %get-tuple-element.7.tiles, bf16[1,2,256,256]{3,2,1,0:T(8,128)(2,1)S(1)} %get-tuple-element.8.diag), custom_call_target="tpu_custom_call" | custom-call | tf_op jit(solution)/shard_map/placed_tiles/pallas_call | solution.py:409

commit v8 on v7

--- a/solution.py
+++ b/solution.py
@@ -198,17 +198,16 @@
         for q in range(ANCESTORS):
             staged[k * ANCESTORS + q] = summed[k, jnp.clip(slot_block(k, q) - 2 * c, 0, 1)]
 
-        def send(step, carry):
-            to = k * ANCESTORS + (c + step) % ANCESTORS
-
-            @pl.when(to != c)
-            def _():
-                pltpu.make_async_remote_copy(
-                    src_ref=staged.at[to], dst_ref=moved.at[c], send_sem=c_send, recv_sem=c_recv,
-                    device_id=(layer, x, to), device_id_type=MESH,
-                ).start()
-            return carry
-        lax.fori_loop(0, ANCESTORS, send, 0)
+        for hop in (2, 1, 3, 0):
+            for row in range(2):
+                to = (2 * k + row) * SIDE + (y + hop) % SIDE
+
+                @pl.when(to != c)
+                def _():
+                    pltpu.make_async_remote_copy(
+                        src_ref=staged.at[to], dst_ref=moved.at[c], send_sem=c_send, recv_sem=c_recv,
+                        device_id=(layer, x, to), device_id_type=MESH,
+                    ).start()
 
     def end_move():
         moved[c] = staged[c]
@@ -232,8 +231,8 @@
     m_copy = to_sibling(panel_t, other_panel_t, m_send, m_recv)
     d_copy = to_sibling(dinv, other_dinv, d_send, d_recv)
 
+    pick_blocks(0)
     gather1.after_first()
-    pick_blocks(0)
     gather1.after_second()
     pick_blocks(1)
     gather1.finish()
@@ -254,9 +253,6 @@
     to_smem.wait()
     start_move(0)
     start_move(1)
-    passed = end_move()
-    gather2.start()
-
     parents, places = [], []
     for k in range(SUPERS):
         parent = parent_of(k)
@@ -268,6 +264,9 @@
             found.append(parent * ANCESTORS + at)
         parents.append(parent)
         places.append(found)
+
+    passed = end_move()
+    gather2.start()
 
     gather2.after_first()
     gather2.after_second()

time: 56.5 us -> 56.1 us (level)
  no operation moved by 1% of the time
where the time goes in v8:
time: 56.1 us; the launch traced here: 56 us
  Pallas kernels  55.4 us (99%)
  between operations  0.64 us (1%)
    pallas_call x1, Pallas kernels, body(): pl.pallas_call(kernel, out_shape=(pltpu.VMEM((SUPERS, ANCESTORS + 1, BLOC...  53.6 us
    pallas_call x1, Pallas kernels, body(): pl.pallas_call(place, out_shape=(jax.ShapeDtypeStruct((1, rows, width), B...  1.76 us

profile of v8, /device:TPU:1, one launch (start us, length us, event | category | flops | bytes accessed | tf_op | source)
XLA Modules:
  0.0 56.0 jit_solution(2220787667518259792)
XLA Ops:
  0.6 53.6 %selected_inverse.1 = (bf16[2,9,256,256]{3,2,1,0:T(8,128)(2,1)S(1)}, bf16[1,2,256,256]{3,2,1,0:T(8,128)(2,1)S(1)}, s32[1,2,8]{2,1,0:T(2,128)S(4)}) custom-call(s32[1,2,8]{2,1,0:T(2,128)} %anc_any.1, bf16[1,64,256]{2,1,0:T(8,128)(2,1)} %panel_any.1, bf16[8,256,512]{2,1,0:T(8,128)(2,1)} %bitcast.1, bf16[1,2,256,256]{3,2,1,0:T(8,128)(2,1)} %dinv_any.1), custom_call_target="tpu_custom_call" | custom-call | tf_op jit(solution)/shard_map/selected_inverse/pallas_call | solution.py:373
  54.2 1.8 %placed_tiles.1 = (bf16[1,2048,512]{2,1,0:T(8,128)(2,1)}, bf16[1,512,512]{2,1,0:T(8,128)(2,1)}, bf16[1,2,256,256]{3,2,1,0:T(8,128)(2,1)}) custom-call(s32[1,2,8]{2,1,0:T(2,128)S(4)} %get-tuple-element.6.anc, bf16[2,9,256,256]{3,2,1,0:T(8,128)(2,1)S(1)} %get-tuple-element.7.tiles, bf16[1,2,256,256]{3,2,1,0:T(8,128)(2,1)S(1)} %get-tuple-element.8.diag), custom_call_target="tpu_custom_call" | custom-call | tf_op jit(solution)/shard_map/placed_tiles/pallas_call | solution.py:408

commit v9 on v8

--- a/solution.py
+++ b/solution.py
@@ -14,6 +14,7 @@
 PIECES = 64
 QUARTER = 64
 SLOTS = SUPERS * ANCESTORS
+HOLDERS = TOP_BLOCKS // 2
 LAST = ANCESTORS - 1
 MESH = pl.DeviceIdType.MESH
 BF16 = jnp.bfloat16
@@ -87,7 +88,7 @@
     other_panel_t, other_dinv, other_piece, anc_in, anc_other, measure,
     in_sem, anc_sem,
     send1, first1, second1, third1, send2, third2,
-    x_send, x_recv, c_send, c_recv, a_send, a_recv, m_send, m_recv, d_send, d_recv,
+    x_send, x_recv, c_send, c_recv, a_send, a_recv, m_send, m_recv, d_send, d_recv, idle_sem,
 ):
     layer = lax.axis_index("layer")
     x = lax.axis_index("prow")
@@ -202,7 +203,7 @@
             for row in range(2):
                 to = (2 * k + row) * SIDE + (y + hop) % SIDE
 
-                @pl.when(to != c)
+                @pl.when(jnp.logical_and(to != c, c < HOLDERS))
                 def _():
                     pltpu.make_async_remote_copy(
                         src_ref=staged.at[to], dst_ref=moved.at[c], send_sem=c_send, recv_sem=c_recv,
@@ -210,9 +211,18 @@
                     ).start()
 
     def end_move():
-        moved[c] = staged[c]
-        wait(c_recv, (PLANE - 1) * PIECE)
-        piece = moved[slot_block(c // ANCESTORS, c % ANCESTORS) // 2]
+        @pl.when(c < HOLDERS)
+        def _():
+            moved[c] = staged[c]
+            wait(c_recv, (HOLDERS - 1) * PIECE)
+            pl.semaphore_wait(idle_sem, PLANE - HOLDERS)
+
+        @pl.when(c >= HOLDERS)
+        def _():
+            wait(c_recv, HOLDERS * PIECE)
+            pl.semaphore_wait(idle_sem, PLANE - HOLDERS - 1)
+
+        piece = moved[jnp.clip(slot_block(c // ANCESTORS, c % ANCESTORS) // 2, 0, HOLDERS - 1)]
         passed = to_sibling(slots.at[z, y, x], other_piece, a_send, a_recv)
 
         @pl.when(layer == 0)
@@ -240,6 +250,13 @@
     start_reduce(0)
     multiply(1)
     start_reduce(1)
+    @pl.when(c >= HOLDERS)
+    def _():
+        for step in range(1, PLANE):
+            pl.semaphore_signal(
+                idle_sem, inc=1, device_id=(layer, x, (c + step) % PLANE), device_id_type=MESH
+            )
+
     turn_panels()
 
     @pl.when(layer == 0)
@@ -317,7 +334,10 @@
     gather1.wait_sent()
     gather2.wait_sent()
     wait(x_send, SUPERS * 3 * 2 * PIECE)
-    wait(c_send, (PLANE - 1) * PIECE)
+
+    @pl.when(c < HOLDERS)
+    def _():
+        wait(c_send, (PLANE - 1) * PIECE)
 
 
 def place(anc, tiles, diag, col_out, row_out, diag_out, zero, col_sem, row_sem, diag_sem):
@@ -389,7 +409,7 @@
             pltpu.VMEM((SUPERS, SIDE - 1, 2, QUARTER, BLOCK), BF16),
             pltpu.VMEM((SUPERS, 2, QUARTER, BLOCK), BF16),
             pltpu.VMEM((SLOTS, QUARTER, BLOCK), BF16),
-            pltpu.VMEM((PLANE, QUARTER, BLOCK), BF16),
+            pltpu.VMEM((HOLDERS, QUARTER, BLOCK), BF16),
             pltpu.VMEM(pieces, BF16),
             pltpu.VMEM((SUPERS, ANCESTORS, BLOCK, BLOCK), BF16),
             pltpu.VMEM(diag_inverse.shape, BF16),
@@ -399,6 +419,7 @@
             pltpu.VMEM((PIECES * PIECE, 16, 128), BF16),
             dma((4,)), dma((2,)), *gather_sems, dma, dma,
             dma, dma((SUPERS,)), dma, dma, dma, dma, dma, dma, dma, dma,
+            pltpu.SemaphoreType.REGULAR,
         ],
         compiler_params=pltpu.CompilerParams(
             collective_id=0, has_side_effects=True, vmem_limit_bytes=VMEM_LIMIT

time: 56.1 us -> 56.2 us (level)
  no operation moved by 1% of the time
where the time goes in v9:
time: 56.2 us; the launch traced here: 56.1 us
  Pallas kernels  55.4 us (99%)
  between operations  0.64 us (1%)
    pallas_call x1, Pallas kernels, body(): pl.pallas_call(kernel, out_shape=(pltpu.VMEM((SUPERS, ANCESTORS + 1, BLOC...  53.7 us
    pallas_call x1, Pallas kernels, body(): pl.pallas_call(place, out_shape=(jax.ShapeDtypeStruct((1, rows, width), B...  1.76 us

profile of v9, /device:TPU:1, one launch (start us, length us, event | category | flops | bytes accessed | tf_op | source)
XLA Modules:
  0.0 56.1 jit_solution(14059751097218750806)
XLA Ops:
  0.6 53.7 %selected_inverse.1 = (bf16[2,9,256,256]{3,2,1,0:T(8,128)(2,1)S(1)}, bf16[1,2,256,256]{3,2,1,0:T(8,128)(2,1)S(1)}, s32[1,2,8]{2,1,0:T(2,128)S(4)}) custom-call(s32[1,2,8]{2,1,0:T(2,128)} %anc_any.1, bf16[1,64,256]{2,1,0:T(8,128)(2,1)} %panel_any.1, bf16[8,256,512]{2,1,0:T(8,128)(2,1)} %bitcast.1, bf16[1,2,256,256]{3,2,1,0:T(8,128)(2,1)} %dinv_any.1), custom_call_target="tpu_custom_call" | custom-call | tf_op jit(solution)/shard_map/selected_inverse/pallas_call | solution.py:393
  54.3 1.8 %placed_tiles.1 = (bf16[1,2048,512]{2,1,0:T(8,128)(2,1)}, bf16[1,512,512]{2,1,0:T(8,128)(2,1)}, bf16[1,2,256,256]{3,2,1,0:T(8,128)(2,1)}) custom-call(s32[1,2,8]{2,1,0:T(2,128)S(4)} %get-tuple-element.6.anc, bf16[2,9,256,256]{3,2,1,0:T(8,128)(2,1)S(1)} %get-tuple-element.7.tiles, bf16[1,2,256,256]{3,2,1,0:T(8,128)(2,1)S(1)} %get-tuple-element.8.diag), custom_call_target="tpu_custom_call" | custom-call | tf_op jit(solution)/shard_map/placed_tiles/pallas_call | solution.py:429

commit v10 on v9

--- a/solution.py
+++ b/solution.py
@@ -309,7 +309,7 @@
     def _():
         m_copy.wait_recv()
         d_copy.wait_recv()
-        crossed, turned = [], []
+        crossed, turned, corners = [], [], []
         for k in range(SUPERS):
             edge = tile_of(panels, k * ANCESTORS + LAST)
             above = other_dinv[0, parents[k]]
@@ -323,12 +323,14 @@
             corner = (-total - crossed[k]).astype(BF16)
             tiles[k, LAST] = corner
             tiles[k, ANCESTORS] = (-total - turned[k]).astype(BF16)
+            corners.append(corner)
+        for k in range(SUPERS):
             total = dinv[0, k].astype(F32)
             for q in range(LAST):
                 tile = tile_of(slots, places[k][q])
                 total -= matrix(panel_t[k, q], tile)
                 tiles[k, q] = tile
-            diag[0, k] = (total - matrix(panel_t[k, LAST], corner)).astype(BF16)
+            diag[0, k] = (total - matrix(panel_t[k, LAST], corners[k])).astype(BF16)
 
     anc_copy.wait_send()
     gather1.wait_sent()

time: 56.2 us -> 56 us (level)
  no operation moved by 1% of the time
where the time goes in v10:
time: 56 us; the launch traced here: 55.9 us
  Pallas kernels  55.2 us (99%)
  between operations  0.64 us (1%)
    pallas_call x1, Pallas kernels, body(): pl.pallas_call(kernel, out_shape=(pltpu.VMEM((SUPERS, ANCESTORS + 1, BLOC...  53.5 us
    pallas_call x1, Pallas kernels, body(): pl.pallas_call(place, out_shape=(jax.ShapeDtypeStruct((1, rows, width), B...  1.76 us

profile of v10, /device:TPU:1, one launch (start us, length us, event | category | flops | bytes accessed | tf_op | source)
XLA Modules:
  0.0 55.9 jit_solution(9665010446036150544)
XLA Ops:
  0.6 53.5 %selected_inverse.1 = (bf16[2,9,256,256]{3,2,1,0:T(8,128)(2,1)S(1)}, bf16[1,2,256,256]{3,2,1,0:T(8,128)(2,1)S(1)}, s32[1,2,8]{2,1,0:T(2,128)S(4)}) custom-call(s32[1,2,8]{2,1,0:T(2,128)} %anc_any.1, bf16[1,64,256]{2,1,0:T(8,128)(2,1)} %panel_any.1, bf16[8,256,512]{2,1,0:T(8,128)(2,1)} %bitcast.1, bf16[1,2,256,256]{3,2,1,0:T(8,128)(2,1)} %dinv_any.1), custom_call_target="tpu_custom_call" | custom-call | tf_op jit(solution)/shard_map/selected_inverse/pallas_call | solution.py:395
  54.1 1.8 %placed_tiles.1 = (bf16[1,2048,512]{2,1,0:T(8,128)(2,1)}, bf16[1,512,512]{2,1,0:T(8,128)(2,1)}, bf16[1,2,256,256]{3,2,1,0:T(8,128)(2,1)}) custom-call(s32[1,2,8]{2,1,0:T(2,128)S(4)} %get-tuple-element.6.anc, bf16[2,9,256,256]{3,2,1,0:T(8,128)(2,1)S(1)} %get-tuple-element.7.tiles, bf16[1,2,256,256]{3,2,1,0:T(8,128)(2,1)S(1)} %get-tuple-element.8.diag), custom_call_target="tpu_custom_call" | custom-call | tf_op jit(solution)/shard_map/placed_tiles/pallas_call | solution.py:431
